TPU v7x, 256 devices: a whole 4x4x8 slice. The times are simulated.
256 devices in a mesh: row: 32 (over z_hi, x, core), col: 8 (over z_lo, y).
Axes of the slice: x: 4, y: 4, z: 8 (z_hi: 4, z_lo: 2; z = z_hi * 2 + z_lo), core: 2. Of those that a mesh axis runs over, the one named last changes fastest.
Arguments:
- support: bfloat16 [16384, 256], P(('row', 'col')), may hold values from -1.5 to 1.5
- support_labels: float32 [15, 16384], P(None, ('row', 'col')), may hold values from -6 to 6
- targets: bfloat16 [65536, 256], P('col'), may hold values from -1.5 to 1.5
- target_labels: float32 [15, 65536], P(None, 'col'), may hold values from -6 to 6
Outputs:
- coefficients: float32 [15, 16384], P(None, ('row', 'col'))
- support_grad: float32 [16384, 256], P(('row', 'col'))
All inputs are finite; a program needn't handle non-finite values.
Results may differ from a plain program's by a relative error of at most 0.0033.
Values may be sent and summed in bfloat16 or wider, within the bound.
A program may use at most 128 MiB of HBM per device.

v0:
```python
import math

import jax
import jax.numpy as jnp
from jax import lax
from jax.sharding import PartitionSpec as P

ITERS = 3


ridge = 0.5


def kernel_block(left, right):
    inner = jnp.dot(left, right.T, preferred_element_type=jnp.float32)
    left_norm = jnp.sum(jnp.square(left.astype(jnp.float32)), axis=1)
    right_norm = jnp.sum(jnp.square(right.astype(jnp.float32)), axis=1)
    return jnp.exp(inner - 0.5 * left_norm[:, None] - 0.5 * right_norm[None, :])


def contract_last(left, right):
    return lax.dot_general(left, right, (((1,), (1,)), ((), ())), precision=lax.Precision.HIGHEST)


def class_sum(left, right):
    return jnp.sum(left * right, axis=1, keepdims=True)


def squares(vector):
    return lax.psum(class_sum(vector, vector), ("row", "col"))


def add_terms(carry, values, rows, error_rows, coef_rows):
    summed, column_sums = carry
    mixing = lax.dot_general(
        error_rows, coef_rows, (((0,), (0,)), ((), ())), precision=lax.Precision.HIGHEST
    )
    weights = (mixing * values).astype(jnp.bfloat16)
    summed = summed + lax.dot_general(
        weights, rows, (((0,), (0,)), ((), ())), preferred_element_type=jnp.float32
    )
    column_sums = column_sums + jnp.sum(weights.astype(jnp.float32), axis=0)
    return (summed, column_sums)


def body(support, support_labels, targets, target_labels):
    row_feats = lax.all_gather(support, "col", axis=0, tiled=True)
    solution = jnp.zeros_like(support_labels)
    residual = support_labels
    direction = support_labels
    norm_now = squares(residual)
    for step in range(ITERS):
        direction_cols = lax.all_gather(direction, "row", axis=1, tiled=True)
        values = kernel_block(row_feats, lax.all_gather(support, "row", axis=0, tiled=True))
        partial_image = contract_last(direction_cols, values)
        image = (
            lax.psum_scatter(partial_image, "col", scatter_dimension=1, tiled=True)
            + ridge * direction
        )
        curve = lax.psum(class_sum(direction, image), ("row", "col"))
        alpha = norm_now / curve
        solution = solution + alpha * direction
        residual = residual - alpha * image
        norm_next = squares(residual)
        direction = residual + norm_next / norm_now * direction
        norm_now = norm_next
    coef_rows = lax.all_gather(solution, "col", axis=1, tiled=True)
    count = targets.shape[0]
    width = math.gcd(count, 512)
    blocks_count = count // width
    target_blocks = targets.reshape(blocks_count, width, targets.shape[1])

    def target_tile(rows):
        return kernel_block(rows, row_feats)

    def predict(rows):
        return contract_last(coef_rows, target_tile(rows))

    partial_pred = jnp.transpose(lax.map(predict, target_blocks), (1, 0, 2)).reshape(
        target_labels.shape
    )
    predictions = lax.psum(partial_pred, "row")
    errors = predictions - target_labels
    error_blocks = jnp.transpose(errors.reshape(errors.shape[0], blocks_count, width), (1, 0, 2))
    initial = (
        jnp.zeros(row_feats.shape, jnp.float32),
        jnp.zeros((row_feats.shape[0],), jnp.float32),
    )

    def accumulate(carry, item):
        rows, error_rows = item
        return (add_terms(carry, target_tile(rows), rows, error_rows, coef_rows), None)

    (summed, column_sums), unused = lax.scan(accumulate, initial, (target_blocks, error_blocks))
    term = summed - column_sums[:, None] * row_feats.astype(jnp.float32)
    total_targets = count * lax.axis_size("col")
    gradient = lax.psum_scatter(term, "col", scatter_dimension=0, tiled=True) / jnp.sqrt(
        jnp.float32(total_targets)
    )
    return (solution, gradient)


def solution(mesh):
    in_specs = (P(("row", "col"), None), P(None, ("row", "col")), P("col", None), P(None, "col"))
    out_specs = (P(None, ("row", "col")), P(("row", "col"), None))
    return jax.shard_map(body, mesh=mesh, in_specs=in_specs, out_specs=out_specs, check_vma=False)
```

profile of v0, /device:TPU:1, one launch (start us, length us, event | category | flops | bytes accessed | tf_op | source)
XLA Modules:
  0.0 1166.2 jit_solution(2105410883259479070)
XLA Ops:
  7.9 49.6 %all-gather = f32[32,64,15]{1,2,0:T(8,128)S(1)} all-gather(f32[1,64,15]{1,2,0:T(8,128)} %bitcast.124), channel_id=1, replica_groups=mesh['row'=32,'col'=8] {'row'}, dimensions={0}, use_global_device_ids=true | all-gather | bytes 126720 | tf_op jit(solution)/shard_map/all_gather | solution.py:53
  57.8 22.7 %all_gather.20 = bf16[512,256]{1,0:T(8,128)(2,1)S(1)} all-gather(bf16[64,256]{1,0:T(8,128)(2,1)} %param.8), channel_id=1, replica_groups=mesh['row'=32,'col'=8] {'col'}, dimensions={0}, use_global_device_ids=true | all-gather | bytes 294912 | tf_op jit(solution)/shard_map/all_gather | solution.py:47
  80.7 1.6 multiply_reduce_fusion.4
  82.3 2.0 subtract_exponential_fusion
  84.3 1.9 copy-done
  86.2 3.6 convolution_bitcast_fusion.3
  90.8 34.1 %reduce-scatter.13.cloned.1.call-done = f32[64,15]{1,0:T(8,128)} async-done(((f32[512,15]{1,0:T(8,128)}), f32[64,15]{1,0:T(8,128)}) %reduce-scatter.13.cloned.1.call-update) | async-done | bytes 3856
  125.9 81.1 %all-reduce = (f32[15,1]{0,1:T(1,128)S(1)}, f32[15,1]{0,1:T(1,128)S(1)}) all-reduce(f32[15,1]{0,1:T(1,128)S(1)} %bitcast.131, f32[15,1]{0,1:T(1,128)S(1)} %bitcast.130), channel_id=1, replica_groups=mesh['row'=32,'col'=8] {'row','col'}, use_global_device_ids=true, to_apply=%region_1.0 | all-reduce | flops 30 | bytes 240 | tf_op jit(solution)/shard_map/psum | solution.py:30
  207.2 72.7 %psum.51 = f32[15,1]{0,1:T(1,128)S(1)} all-reduce(f32[15,1]{0,1:T(1,128)S(1)} %bitcast.133), channel_id=1, replica_groups=mesh['row'=32,'col'=8] {'row','col'}, use_global_device_ids=true, to_apply=%region_8.0 | all-reduce | flops 15 | bytes 120 | tf_op jit(solution)/shard_map/psum | solution.py:30
  279.9 42.8 %all-gather.1 = f32[32,64,15]{1,2,0:T(8,128)S(1)} all-gather(f32[1,64,15]{1,2,0:T(8,128)S(1)} %bitcast.123), channel_id=1, replica_groups=mesh['row'=32,'col'=8] {'row'}, dimensions={0}, use_global_device_ids=true | all-gather | bytes 126720 | tf_op jit(solution)/shard_map/all_gather | solution.py:53
  323.0 6.3 convolution_bitcast_fusion.2
  329.3 28.3 %reduce-scatter.15.cloned.1.call-done = f32[64,15]{1,0:T(8,128)} async-done(((f32[512,15]{1,0:T(8,128)}), f32[64,15]{1,0:T(8,128)}) %reduce-scatter.15.cloned.1.call-update) | async-done | bytes 3856
  358.6 81.3 %psum.52 = f32[15,1]{0,1:T(1,128)S(1)} all-reduce(f32[15,1]{0,1:T(1,128)S(1)} %bitcast.134), channel_id=1, replica_groups=mesh['row'=32,'col'=8] {'row','col'}, use_global_device_ids=true, to_apply=%region_11.0 | all-reduce | flops 15 | bytes 120 | tf_op jit(solution)/shard_map/psum | solution.py:60
  440.1 72.7 %psum.53 = f32[15,1]{0,1:T(1,128)S(1)} all-reduce(f32[15,1]{0,1:T(1,128)S(1)} %bitcast.129), channel_id=1, replica_groups=mesh['row'=32,'col'=8] {'row','col'}, use_global_device_ids=true, to_apply=%region_13.0 | all-reduce | flops 15 | bytes 120 | tf_op jit(solution)/shard_map/psum | solution.py:30
  512.9 42.9 %all-gather.2 = f32[32,64,15]{1,2,0:T(8,128)S(1)} all-gather(f32[1,64,15]{1,2,0:T(8,128)S(1)} %fusion.17), channel_id=1, replica_groups=mesh['row'=32,'col'=8] {'row'}, dimensions={0}, use_global_device_ids=true | all-gather | bytes 126720 | tf_op jit(solution)/shard_map/all_gather | solution.py:53
  555.9 6.3 convolution_bitcast_fusion.1
  562.2 28.3 %reduce-scatter.17.cloned.1.call-done = f32[64,15]{1,0:T(8,128)} async-done(((f32[512,15]{1,0:T(8,128)}), f32[64,15]{1,0:T(8,128)}) %reduce-scatter.17.cloned.1.call-update) | async-done | bytes 3856
  591.5 81.1 %psum.54 = f32[15,1]{0,1:T(1,128)S(1)} all-reduce(f32[15,1]{0,1:T(1,128)S(1)} %bitcast.132), channel_id=1, replica_groups=mesh['row'=32,'col'=8] {'row','col'}, use_global_device_ids=true, to_apply=%region_16.0 | all-reduce | flops 15 | bytes 120 | tf_op jit(solution)/shard_map/psum | solution.py:60
  672.7 21.8 %all-gather.3 = f32[8,64,15]{1,2,0:T(8,128)S(1)} all-gather(f32[1,64,15]{1,2,0:T(8,128)S(1)} %bitcast.125), channel_id=1, replica_groups=mesh['row'=32,'col'=8] {'col'}, dimensions={0}, use_global_device_ids=true | all-gather | bytes 34560 | tf_op jit(solution)/shard_map/all_gather | solution.py:67
  694.7 56.2 %while.23 = (s32[]{:T(128)}, f32[16,15,512]{2,1,0:T(8,128)S(1)}, bf16[16,512,256]{2,1,0:T(8,128)(2,1)}, bf16[512,256]{1,0:T(8,128)(2,1)S(1)}, f32[15,512]{1,0:T(8,128)S(1)}, /*index=5*/s32[]{:T(128)}) while((s32[]{:T(128)}, f32[16,15,512]{2,1,0:T(8,128)S(1)}, bf16[16,512,256]{2,1,0:T(8,128)(2,1)}, bf16[512,256]{1,0:T(8,128)(2,1)S(1)}, ...), condition=%wide.region_20.0_spmd, body=%wide.region_17.20_spmd.sunk | while | flops 182714368 | bytes 3228237 | solution.py:79
  752.5 287.2 %all-reduce.3.cloned.1.call-done = f32[15,8192]{1,0:T(8,128)} async-done(((f32[15,8192]{1,0:T(8,128)}), f32[15,8192]{1,0:T(8,128)}) %all-reduce.3.cloned.1.call-update) | async-done | bytes 491536 | tf_op jit(solution)/shard_map/psum | solution.py:82
  1041.1 81.3 %while.24 = (s32[]{:T(128)}, f32[512,256]{1,0:T(8,128)S(1)}, f32[512]{0:T(512)S(1)}, f32[16,15,512]{2,0,1:T(8,128)S(1)}, f32[15,512]{1,0:T(8,128)S(1)}, /*index=...) while((s32[]{:T(128)}, f32[512,256]{1,0:T(8,128)S(1)}, ...), condition=%wide.region_26.27_spmd.clone, body=%wide.region_22.26_spmd.clone.sunk | while | flops 318243328 | bytes 5653616 | solution.py:94
  1049.8 1.4 convolution_add_fusion.2
  1054.9 1.4 convolution_add_fusion.2
  1065.1 1.4 convolution_add_fusion.2
  1070.2 1.4 convolution_add_fusion.2
  1080.3 1.4 convolution_add_fusion.2
  1095.6 1.4 convolution_add_fusion.2
  1100.6 1.4 convolution_add_fusion.2
  1115.9 1.4 convolution_add_fusion.2
  1123.3 34.5 %reduce-scatter.11.cloned.1.call-done = f32[64,256]{1,0:T(8,128)} async-done(((f32[512,256]{1,0:T(8,128)}), f32[64,256]{1,0:T(8,128)}) %reduce-scatter.11.cloned.1.call-update) | async-done | bytes 65552 | tf_op jit(solution)/shard_map/reduce_scatter | solution.py:97
  1157.8 1.5 broadcast_multiply_fusion.4
  (258 shorter events, 135.0 us)
Async XLA Ops:
  7.2 73.5 %all-gather.6.cloned.1.call-start = ((), (), s32[]{:S(2)}) async-start(), calls=%async_computation.4 | async-start | bytes 1081344 | tf_op jit(solution)/shard_map/all_gather | solution.py:54
  7.9 117.0 %reduce-scatter.13.cloned.1.call-start = ((), (), s32[]{:S(2)}) async-start(), calls=%async_computation.7 | async-start | bytes 294912
  82.3 43.5 %copy-start.2 = (f32[15,64]{1,0:T(8,128)S(1)}, f32[15,64]{1,0:T(8,128)}, u32[]{:S(2)}) copy-start(f32[15,64]{1,0:T(8,128)} %param.9) | copy-start | bytes 11524
  84.3 1.9 copy-start
  90.7 266.9 %reduce-scatter.15.cloned.1.call-start = ((), (), s32[]{:S(2)}) async-start(), calls=%async_computation.8 | async-start | bytes 294912
  329.2 261.3 %reduce-scatter.17.cloned.1.call-start = ((), (), s32[]{:S(2)}) async-start(), calls=%async_computation.9 | async-start | bytes 294912
  562.2 477.4 %all-reduce.3.cloned.1.call-start = ((), (), s32[]{:S(2)}) async-start(), calls=%async_computation.5 | async-start | bytes 1048576 | tf_op jit(solution)/shard_map/psum | solution.py:82
  672.7 21.9 %copy-start.3 = (f32[15,64]{1,0:T(8,128)}, f32[15,64]{1,0:T(8,128)S(1)}, u32[]{:S(2)}) copy-start(f32[15,64]{1,0:T(8,128)S(1)} %multiply_add_fusion) | copy-start | bytes 11524
  694.7 345.0 %copy-start.1 = (f32[15,8192]{1,0:T(8,128)S(1)}, f32[15,8192]{1,0:T(8,128)}, u32[]{:S(2)}) copy-start(f32[15,8192]{1,0:T(8,128)} %param.11) | copy-start | bytes 1474564
  752.4 405.4 %reduce-scatter.11.cloned.1.call-start = ((), (), s32[]{:S(2)}) async-start(), calls=%async_computation.6 | async-start | bytes 589824 | tf_op jit(solution)/shard_map/reduce_scatter | solution.py:97
Sparse Core Ops, SparseCore 0:
  10.6 56.6 all-gather.5
  90.9 34.0 reduce-scatter.12
  329.4 28.2 reduce-scatter.14
  562.3 28.1 reduce-scatter.16
  752.5 287.0 all-reduce.2
  1123.5 34.3 reduce-scatter.10
where the time goes:
time: 1170 us
  blocking collectives  569 us (49%)
  waiting for transfers between devices  413 us (35%)
  matrix products  116 us (10%)
  other arithmetic  44.4 us (4%)
  between operations  14.3 us (1%)
    psum x1, waiting for transfers between devices, body(): predictions = lax.psum(partial_pred, 'row')  287 us
    psum x3, blocking collectives, squares(): return lax.psum(class_sum(vector, vector), ('row', 'col'))  226 us
    psum x2, blocking collectives, body(): curve = lax.psum(class_sum(direction, image), ('row', 'col'))  162 us
    all_gather x3, blocking collectives, body(): direction_cols = lax.all_gather(direction, 'row', axis=1, tiled=True)  135 us
    unnamed x9, waiting for transfers between devices  91.5 us
    dot_general x33, matrix products, kernel_block(): inner = jnp.dot(left, right.T, preferred_element_type=jnp.float32)  43.8 us
    reduce_sum x33, other arithmetic, kernel_block(): right_norm = jnp.sum(jnp.square(right.astype(jnp.float32)), axis=1)  39.2 us
    reduce_scatter x1, waiting for transfers between devices, body(): lax.psum_scatter(term, 'col', scatter_dimension=0, tiled=True)  34.5 us
  transfers between devices with their start and end apart: 6, of which 5 were waited for; matrix products, arithmetic and copies ran while one was open for 0% of the time, Pallas kernels for 0%

commit v1 on v0

v1 whole, which is shorter than its diff:
```python
import jax
import jax.numpy as jnp
from jax import lax
from jax.experimental import pallas as pl
from jax.experimental.pallas import tpu as pltpu
from jax.sharding import PartitionSpec as P

MESH = pl.DeviceIdType.MESH
F32 = jnp.float32
BF16 = jnp.bfloat16

CHUNK = 64
FEAT = 256
TILE = 256
TILES = 32
GROUP = 16
WIDE = GROUP * CHUNK
HALF = WIDE // 2
RIDGE = 0.5
NN = (((1,), (0,)), ((), ()))
NT = (((1,), (1,)), ((), ()))


def dot(a, b, dims=NN):
    return lax.dot_general(a, b, dims, preferred_element_type=F32)


def split3(v):
    hi = v.astype(BF16)
    rest = v - hi.astype(F32)
    mid = rest.astype(BF16)
    low = (rest - mid.astype(F32)).astype(BF16)
    return hi, mid, low


def row_norms(rows):
    square = jnp.square(rows.astype(F32))
    hi = square.astype(BF16)
    low = (square - hi.astype(F32)).astype(BF16)
    ones = jnp.ones((8, FEAT), BF16)
    return 0.5 * (dot(ones, hi, NT) + dot(ones, low, NT))[0:1, :]


def column_norms(rows):
    return 0.5 * jnp.sum(jnp.square(rows.astype(F32)), axis=1, keepdims=True)


def pack_pair(v):
    left = lax.broadcasted_iota(jnp.int32, (8, 128), 1) < CHUNK
    top, bottom = v[0:8], v[8:16]
    first = jnp.where(left, top, pltpu.roll(bottom, CHUNK, 1))
    second = jnp.where(left, pltpu.roll(top, CHUNK, 1), bottom)
    return first, second


def unpack_pair(a, b):
    left = lax.broadcasted_iota(jnp.int32, (8, 128), 1) < CHUNK
    top = jnp.where(left, a, pltpu.roll(b, CHUNK, 1))
    bottom = jnp.where(left, pltpu.roll(a, CHUNK, 1), b)
    return jnp.concatenate([top, bottom], axis=0)


def unpack(ref):
    wide = jnp.concatenate([unpack_pair(ref[2 * j], ref[2 * j + 1]) for j in range(GROUP // 2)], axis=1)
    return jnp.where(lax.broadcasted_iota(jnp.int32, wide.shape, 0) < 15, wide, 0.0)


def to_lanes(q, shift):
    sub = lax.broadcasted_iota(jnp.int32, (16, 128), 0)
    lane = lax.broadcasted_iota(jnp.int32, (16, 128), 1)
    return jnp.sum(jnp.where(lane == sub + shift, q, 0.0), axis=0, keepdims=True)


def from_lanes(row, shift):
    sub = lax.broadcasted_iota(jnp.int32, (16, 128), 0)
    lane = lax.broadcasted_iota(jnp.int32, (16, 128), 1)
    return jnp.sum(jnp.where(lane == sub + shift, row, 0.0), axis=1, keepdims=True)


def put_scalars(message, row):
    sub = lax.broadcasted_iota(jnp.int32, (8, 128), 0)
    lane = lax.broadcasted_iota(jnp.int32, (8, 128), 1)
    return jnp.where((sub == 7) & (lane >= CHUNK), row, message)


def lane_sum(v):
    return jnp.sum(v, axis=1, keepdims=True)


def ratio(a, b):
    real = lax.broadcasted_iota(jnp.int32, (16, 1), 0) < 15
    return jnp.where(real, a, 0.0) / jnp.where(real, b, 1.0)


def tree(values):
    values = list(values)
    while len(values) > 1:
        values = [values[i] + values[i + 1] if i + 1 < len(values) else values[i] for i in range(0, len(values), 2)]
    return values[0]


def kernel(
    sup_ref, lab_ref, tgt_hbm, tlab_hbm,
    coef_ref, grad_ref,
    tgt, tlab, rf, cf, sup_v, lab_rows, lab_cols,
    kt_hi, kt_lo, kk_hi, kk_lo, sn_ref,
    s1_send, s1_recv, s2_send, s2_rows, s2_cols, s3_send, s3_recv,
    drow, rrow, xrow, dcol, rcol, prev,
    pred_send, pred_recv, err_own, err, xt, gsum, csum, g_send, g_recv,
    local_sems, f_send, f_recv, l_send, l_recv, v_send, v_recv, pred_ss, pred_rs, err_ss, err_rs, g_ss, g_rs,
):
    r = lax.axis_index("row")
    c = lax.axis_index("col")
    chip, core = r // 2, lax.rem(r, 2)
    z, x = chip // 4, lax.rem(chip, 4)
    me = core * 8 + c

    def row_peer(i):
        p = lax.rem(me + i, GROUP)
        return (2 * chip + p // 8, lax.rem(p, 8))

    def col_peer(i):
        return (2 * lax.rem(chip + i, GROUP) + core, c)

    tgt_copy = pltpu.make_async_copy(tgt_hbm, tgt, local_sems.at[0])
    tgt_copy.start()
    start_lane = pl.multiple_of(r * TILE, TILE)
    tlab_copy = pltpu.make_async_copy(tlab_hbm.at[:, pl.ds(start_lane, TILE)], tlab, local_sems.at[1])
    tlab_copy.start()

    barrier = pltpu.get_barrier_semaphore()

    @pl.loop(1, GROUP)
    def _(i):
        pl.semaphore_signal(barrier, inc=1, device_id=row_peer(i), device_id_type=MESH)

    @pl.loop(1, 32)
    def _(i):
        q = lax.rem(r + i, 32)

        @pl.when(q // 2 != chip)
        def _():
            pl.semaphore_signal(barrier, inc=1, device_id=(q, c), device_id_type=MESH)

    sup = sup_ref[...]
    rf[me] = sup
    cf[chip] = sup
    sup_v[...] = sup
    lab = jnp.concatenate([lab_ref[...], jnp.zeros((1, CHUNK), F32)], axis=0)
    packed = jnp.concatenate([lab[0:8], lab[8:16]], axis=1)
    s2_send[0] = packed
    lab_rows[me] = packed
    lab_cols[chip] = packed

    pl.semaphore_wait(barrier, 45)

    def remote(src, dst, ss, rs, to):
        return pltpu.make_async_remote_copy(
            src_ref=src, dst_ref=dst, send_sem=ss, recv_sem=rs, device_id=to, device_id_type=MESH
        )

    def wait_for(ref, sem):
        pltpu.make_async_copy(ref, ref, sem).wait()

    @pl.loop(1, GROUP)
    def _(i):
        remote(sup_v, rf.at[me], f_send.at[0], f_recv.at[0], row_peer(i)).start()

    @pl.loop(1, 4)
    def _(i):
        remote(sup_v, cf.at[chip], f_send.at[1], f_recv.at[1], (2 * (lax.rem(z + i, 4) * 4 + x) + core, c)).start()

    @pl.loop(1, GROUP)
    def _(i):
        remote(s2_send.at[0], lab_rows.at[me], l_send.at[0], l_recv.at[0], row_peer(i)).start()
        remote(s2_send.at[0], lab_cols.at[chip], l_send.at[1], l_recv.at[1], col_peer(i)).start()

    wait_for(cf.at[pl.ds(0, 3)], f_recv.at[1])

    @pl.loop(1, 4)
    def _(i):
        to = (2 * (z * 4 + lax.rem(x + i, 4)) + core, c)

        @pl.loop(0, 4)
        def _(j):
            remote(cf.at[j * 4 + x], cf.at[j * 4 + x], f_send.at[2], f_recv.at[2], to).start()

    wait_for(rf.at[pl.ds(0, 15)], f_recv.at[0])
    tgt_copy.wait()
    rows512 = rf[pl.ds(core * 8, 8)].reshape(HALF, FEAT)
    sn_ref[...] = column_norms(rows512)

    def target_tile(i):
        rows = tgt[i]
        inner = dot(rf[pl.ds(core * 8, 8)].reshape(HALF, FEAT), rows, NT)
        value = jnp.exp(inner - sn_ref[...] - row_norms(rows))
        hi = value.astype(BF16)
        kk_hi[i] = hi
        kk_lo[i] = (value - hi.astype(F32)).astype(BF16)

    done = [0]

    def fill(count):
        stop = min(TILES, done[0] + count)
        if stop > done[0]:
            pl.loop(done[0], stop)(target_tile)
        done[0] = stop

    fill(10)

    wait_for(cf.at[pl.ds(0, 12)], f_recv.at[2])
    rows_all = rf[...].reshape(WIDE, FEAT)
    prev[0:1, :] = row_norms(rows_all)

    @pl.loop(0, 4)
    def _(j):
        part = cf[pl.ds(j * 4, 4)].reshape(TILE, FEAT)
        inner = dot(part, rf[...].reshape(WIDE, FEAT), NT)
        value = jnp.exp(inner - column_norms(part) - prev[0:1, :])
        hi = value.astype(BF16)
        where = pl.ds(pl.multiple_of(j * TILE, TILE), TILE)
        kt_hi[where, :] = hi
        kt_lo[where, :] = (value - hi.astype(F32)).astype(BF16)

    def apply_tile(v):
        hi, mid, low = split3(v)
        big = dot(jnp.concatenate([hi, mid, low], axis=0), kt_hi[...])
        small = dot(jnp.concatenate([hi, mid], axis=0), kt_lo[...])
        return (big[0:16] + small[0:16]) + ((big[16:32] + small[16:32]) + big[32:48])

    wait_for(lab_rows.at[pl.ds(0, 15)], l_recv.at[0])
    wait_for(lab_cols.at[pl.ds(0, 15)], l_recv.at[1])
    b_rows = unpack(lab_rows)
    b_cols = unpack(lab_cols)
    drow[...] = b_rows
    rrow[...] = b_rows
    xrow[...] = jnp.zeros_like(b_rows)
    dcol[...] = b_cols
    rcol[...] = b_cols
    rr = None

    waits = ((4, 4), (4, 4), (3, 3))
    for step in range(3):
        last = step == 2
        applied = apply_tile(rcol[...])
        if step > 0:
            wait_for(s3_recv.at[step - 1, pl.ds(0, 15)], v_recv.at[step - 1, 3])
            new = from_lanes(tree([s3_recv[step - 1, j] for j in range(GROUP)])[7:8], CHUNK)
            beta = ratio(new, rr)
            rr = new
            applied = applied + beta * prev[...]
            drow[...] = rrow[...] + beta * drow[...]
            dcol[...] = rcol[...] + beta * dcol[...]
        prev[...] = applied
        d = drow[...]
        scalars = to_lanes(lane_sum(d * (applied + (RIDGE / GROUP) * d)), CHUNK)
        if step == 0:
            scalars = scalars + to_lanes(lane_sum(d * d) * (1.0 / GROUP), CHUNK + 16)
        if last:
            s1_send[step, 0] = put_scalars(jnp.zeros((8, 128), F32), scalars)
            s1_recv[step, me] = s1_send[step, 0]

            @pl.loop(1, GROUP)
            def _(i):
                remote(s1_send.at[step, 0], s1_recv.at[step, me], v_send.at[step, 0], v_recv.at[step, 0], row_peer(i)).start()
        else:
            for j in range(GROUP // 2):
                first, second = pack_pair(applied[:, 128 * j:128 * (j + 1)])
                s1_send[step, 2 * j] = put_scalars(first, scalars)
                s1_send[step, 2 * j + 1] = put_scalars(second, scalars)
            s1_recv[step, me] = s1_send[step, me]

            @pl.loop(1, GROUP)
            def _(i):
                p = lax.rem(me + i, GROUP)
                remote(s1_send.at[step, p], s1_recv.at[step, me], v_send.at[step, 0], v_recv.at[step, 0], row_peer(i)).start()

        fill(waits[step][0])
        wait_for(s1_recv.at[step, pl.ds(0, 15)], v_recv.at[step, 0])
        own = tree([s1_recv[step, j] for j in range(GROUP)])
        s2_send[1 + step] = own
        s2_cols[step, chip] = own
        if not last:
            s2_rows[step, me] = own

        @pl.loop(1, GROUP)
        def _(i):
            remote(s2_send.at[1 + step], s2_cols.at[step, chip], v_send.at[step, 1], v_recv.at[step, 1], col_peer(i)).start()
            if not last:
                remote(s2_send.at[1 + step], s2_rows.at[step, me], v_send.at[step, 2], v_recv.at[step, 2], row_peer(i)).start()

        fill(waits[step][1])
        wait_for(s2_cols.at[step, pl.ds(0, 15)], v_recv.at[step, 1])
        total = tree([s2_cols[step, j] for j in range(GROUP)])[7:8]
        if step == 0:
            rr = from_lanes(total, CHUNK + 16)
        alpha = ratio(rr, from_lanes(total, CHUNK))
        xrow[...] = xrow[...] + alpha * drow[...]
        if not last:
            y_cols = unpack(s2_cols.at[step]) + RIDGE * dcol[...]
            left = rcol[...] - alpha * y_cols
            rcol[...] = left
            s3_send[step] = put_scalars(jnp.zeros((8, 128), F32), to_lanes(lane_sum(left * left), CHUNK))
            s3_recv[step, me] = s3_send[step]

            @pl.loop(1, GROUP)
            def _(i):
                remote(s3_send.at[step], s3_recv.at[step, me], v_send.at[step, 3], v_recv.at[step, 3], row_peer(i)).start()

            wait_for(s2_rows.at[step, pl.ds(0, 15)], v_recv.at[step, 2])
            rrow[...] = rrow[...] - alpha * (unpack(s2_rows.at[step]) + RIDGE * drow[...])

    fill(TILES)

    pair = xrow[:, pl.ds(pl.multiple_of((me // 2) * 128, 128), 128)]
    own_x = jnp.where(lax.rem(me, 2) == 0, pair, pltpu.roll(pair, CHUNK, 1))
    coef_ref[...] = own_x[0:15, 0:CHUNK]

    x512 = xrow[:, pl.ds(pl.multiple_of(core * HALF, HALF), HALF)]
    hi, mid, low = split3(x512)
    x48 = jnp.concatenate([hi, mid, low], axis=0)
    x32 = jnp.concatenate([hi, mid], axis=0)
    wide = jnp.concatenate([hi.astype(F32), mid.astype(F32), jnp.zeros((96, HALF), F32)], axis=0)
    xt[...] = wide.T[:, 0:32].astype(BF16)

    def predict(i):
        big = dot(x48, kk_hi[i])
        small = dot(x32, kk_lo[i])
        return (big[0:16] + small[0:16]) + ((big[16:32] + small[16:32]) + big[32:48])

    @pl.loop(1, TILES)
    def _(i):
        t = lax.rem(r + i, TILES)
        pred_send[t] = predict(t)
        remote(pred_send.at[t], pred_recv.at[r], pred_ss, pred_rs, (t, c)).start()

    pred_recv[r] = predict(r)
    tlab_copy.wait()
    wait_for(pred_recv.at[pl.ds(0, 31)], pred_rs)
    labels = jnp.concatenate([tlab[...], jnp.zeros((1, TILE), F32)], axis=0)
    own_err = (tree([pred_recv[j] for j in range(TILES)]) - labels).astype(BF16)
    err_own[...] = own_err
    err[r] = own_err

    @pl.loop(1, TILES)
    def _(i):
        t = lax.rem(r + i, TILES)
        remote(err_own, err.at[r], err_ss, err_rs.at[r], (t, c)).start()

    gsum[...] = jnp.zeros_like(gsum)
    csum[...] = jnp.zeros_like(csum)

    def accumulate(t):
        e = err[t]
        mix = dot(xt[...], jnp.concatenate([e, e], axis=0))
        weights = (mix * kk_hi[t].astype(F32)).astype(BF16)
        gsum[...] += dot(weights, tgt[t])
        back = weights.astype(F32)
        csum[...] += back[:, 0:128] + back[:, 128:256]

    accumulate(r)

    @pl.loop(1, TILES)
    def _(i):
        t = lax.rem(r + TILES - i, TILES)
        wait_for(err.at[t], err_rs.at[t])
        accumulate(t)

    scale = 1.0 / 256.0
    sums = lane_sum(csum[...])
    term = (gsum[...] - sums * rf[pl.ds(core * 8, 8)].reshape(HALF, FEAT).astype(F32)) * scale
    g_send[...] = term.reshape(8, CHUNK, FEAT)
    g_recv[c] = g_send[c]

    @pl.loop(1, 8)
    def _(i):
        p = lax.rem(c + i, 8)
        remote(g_send.at[p], g_recv.at[c], g_ss, g_rs, (r, p)).start()

    wait_for(g_recv.at[pl.ds(0, 7)], g_rs)
    grad_ref[...] = tree([g_recv[j] for j in range(8)])

    wait_for(rf.at[pl.ds(0, 15)], f_send.at[0])
    wait_for(cf.at[pl.ds(0, 3)], f_send.at[1])
    wait_for(cf.at[pl.ds(0, 12)], f_send.at[2])
    wait_for(lab_rows.at[pl.ds(0, 15)], l_send.at[0])
    wait_for(lab_cols.at[pl.ds(0, 15)], l_send.at[1])
    for step in range(3):
        wait_for(s1_recv.at[step, pl.ds(0, 15)], v_send.at[step, 0])
        wait_for(s2_cols.at[step, pl.ds(0, 15)], v_send.at[step, 1])
        if step < 2:
            wait_for(s2_rows.at[step, pl.ds(0, 15)], v_send.at[step, 2])
            wait_for(s3_recv.at[step, pl.ds(0, 15)], v_send.at[step, 3])
    wait_for(pred_recv.at[pl.ds(0, 31)], pred_ss)
    wait_for(err.at[pl.ds(0, 31)], err_ss)
    wait_for(g_recv.at[pl.ds(0, 7)], g_ss)


def body(support, support_labels, targets, target_labels):
    classes = support_labels.shape[0]
    vmem = pl.BlockSpec(memory_space=pltpu.VMEM)
    anywhere = pl.BlockSpec(memory_space=pl.ANY)
    dma = pltpu.SemaphoreType.DMA
    return pl.pallas_call(
        kernel,
        out_shape=(
            jax.ShapeDtypeStruct((classes, CHUNK), F32),
            jax.ShapeDtypeStruct((CHUNK, FEAT), F32),
        ),
        in_specs=[vmem, vmem, anywhere, anywhere],
        out_specs=(vmem, vmem),
        scratch_shapes=[
            pltpu.VMEM((TILES, TILE, FEAT), BF16),
            pltpu.VMEM((classes, TILE), F32),
            pltpu.VMEM((GROUP, CHUNK, FEAT), BF16),
            pltpu.VMEM((GROUP, CHUNK, FEAT), BF16),
            pltpu.VMEM((CHUNK, FEAT), BF16),
            pltpu.VMEM((GROUP, 8, 128), F32),
            pltpu.VMEM((GROUP, 8, 128), F32),
            pltpu.VMEM((WIDE, WIDE), BF16),
            pltpu.VMEM((WIDE, WIDE), BF16),
            pltpu.VMEM((TILES, HALF, TILE), BF16),
            pltpu.VMEM((TILES, HALF, TILE), BF16),
            pltpu.VMEM((HALF, 1), F32),
            pltpu.VMEM((3, GROUP, 8, 128), F32),
            pltpu.VMEM((3, GROUP, 8, 128), F32),
            pltpu.VMEM((4, 8, 128), F32),
            pltpu.VMEM((2, GROUP, 8, 128), F32),
            pltpu.VMEM((3, GROUP, 8, 128), F32),
            pltpu.VMEM((2, 8, 128), F32),
            pltpu.VMEM((2, GROUP, 8, 128), F32),
            pltpu.VMEM((GROUP, WIDE), F32),
            pltpu.VMEM((GROUP, WIDE), F32),
            pltpu.VMEM((GROUP, WIDE), F32),
            pltpu.VMEM((GROUP, WIDE), F32),
            pltpu.VMEM((GROUP, WIDE), F32),
            pltpu.VMEM((GROUP, WIDE), F32),
            pltpu.VMEM((TILES, GROUP, TILE), F32),
            pltpu.VMEM((TILES, GROUP, TILE), F32),
            pltpu.VMEM((GROUP, TILE), BF16),
            pltpu.VMEM((TILES, GROUP, TILE), BF16),
            pltpu.VMEM((HALF, 32), BF16),
            pltpu.VMEM((HALF, FEAT), F32),
            pltpu.VMEM((HALF, 128), F32),
            pltpu.VMEM((8, CHUNK, FEAT), F32),
            pltpu.VMEM((8, CHUNK, FEAT), F32),
            dma((2,)),
            dma((3,)),
            dma((3,)),
            dma((2,)),
            dma((2,)),
            dma((3, 4)),
            dma((3, 4)),
            dma,
            dma,
            dma,
            dma((TILES,)),
            dma,
            dma,
        ],
        compiler_params=pltpu.CompilerParams(
            collective_id=0, has_side_effects=True, vmem_limit_bytes=58 * 1024 * 1024
        ),
    )(support, support_labels, targets.reshape(TILES, TILE, FEAT), target_labels)


def solution(mesh):
    in_specs = (P(("row", "col"), None), P(None, ("row", "col")), P("col", None), P(None, "col"))
    out_specs = (P(None, ("row", "col")), P(("row", "col"), None))
    return jax.shard_map(body, mesh=mesh, in_specs=in_specs, out_specs=out_specs, check_vma=False)
```

time: 1170 us -> 123 us (0.11)
  blocking collectives: 569 us -> 0 us
  waiting for transfers between devices: 413 us -> 0 us
  Pallas kernels: 0 us -> 119 us
  matrix products: 116 us -> 0 us
  other arithmetic: 44.4 us -> 0 us
  between operations: 14.3 us -> 0.64 us
    psum x5 -> x0, blocking collectives: 389 us -> none  [the longest x3 226 us: squares(): return lax.psum(class_sum(vector, vector), ('row', 'col'))]
    psum x1 -> x0, waiting for transfers between devices: 287 us -> none  [body(): predictions = lax.psum(partial_pred, 'row')]
    all_gather x5 -> x0, blocking collectives: 180 us -> none  [the longest x3 135 us: body(): direction_cols = lax.all_gather(direction, 'row', axis=1, tiled=True)]
    pallas_call x0 -> x1, Pallas kernels: none -> 119 us  [body(): pl.pallas_call(kernel, out_shape=(jax.ShapeDtypeStruct((classes, CHUNK),...]
    dot_general x82 -> x0, matrix products: 103 us -> none  [the longest x33 43.8 us: kernel_block(): inner = jnp.dot(left, right.T, preferred_element_type=jnp.float32)]
    unnamed x9 -> x0, waiting for transfers between devices: 91.5 us -> none
    reduce_sum x39 -> x0, other arithmetic: 40.2 us -> none  [the longest x33 39.2 us: kernel_block(): right_norm = jnp.sum(jnp.square(right.astype(jnp.float32)), axis=1)]
    reduce_scatter x1 -> x0, waiting for transfers between devices: 34.5 us -> none  [body(): lax.psum_scatter(term, 'col', scatter_dimension=0, tiled=True)]
  transfers between devices with their start and end apart: 6 -> 0, of which waited for: 5 -> 0; matrix products, arithmetic and copies ran while one was open for 0% -> 0% of each run, Pallas kernels for 0% -> 0%
where the time goes in v1:
time: 123 us
  Pallas kernels  119 us (97%)
  local copies, waits for them, and re-layouts  2.77 us (2%)
    pallas_call x1, Pallas kernels, body(): pl.pallas_call(kernel, out_shape=(jax.ShapeDtypeStruct((classes, CHUNK),...  119 us
    unnamed x2, local copies, waits for them, and re-layouts  2.77 us

profile of v1, /device:TPU:1, one launch (start us, length us, event | category | flops | bytes accessed | tf_op | source)
XLA Modules:
  0.0 122.7 jit_solution(2546473476684645841)
XLA Ops:
  0.6 119.3 %shard_map.59 = (f32[15,64]{1,0:T(8,128)}, f32[64,256]{1,0:T(8,128)}) custom-call(bf16[64,256]{1,0:T(8,128)(2,1)} %sup_ref.1, f32[15,64]{1,0:T(8,128)} %lab_ref.1, bf16[32,256,256]{2,1,0:T(8,128)(2,1)} %bitcast.1, f32[15,8192]{1,0:T(8,128)} %tlab_hbm.1), custom_call_target="tpu_custom_call" | custom-call | tf_op jit(solution)/shard_map/pallas_call | solution.py:404
  120.0 1.3 %copy.8 = f32[15,64]{1,0:T(8,128)} copy(f32[15,64]{1,0:T(8,128)} %get-tuple-element.4) | data formatting | bytes 7680
  121.3 1.5 %copy.9 = f32[64,256]{1,0:T(8,128)} copy(f32[64,256]{1,0:T(8,128)} %get-tuple-element.5) | data formatting | bytes 131072

commit v2 on v1

v2 whole, which is shorter than its diff:
```python
import jax
import jax.numpy as jnp
from jax import lax
from jax.experimental import pallas as pl
from jax.experimental.pallas import tpu as pltpu
from jax.sharding import PartitionSpec as P

MESH = pl.DeviceIdType.MESH
F32 = jnp.float32
BF16 = jnp.bfloat16

CHUNK = 64
FEAT = 256
TILE = 256
TILES = 32
GROUP = 16
WIDE = GROUP * CHUNK
HALF = WIDE // 2
RIDGE = 0.5
UNIT = CHUNK + 16
NN = (((1,), (0,)), ((), ()))
NT = (((1,), (1,)), ((), ()))


def dot(a, b, dims=NN):
    return lax.dot_general(a, b, dims, preferred_element_type=F32)


def split3(v):
    hi = v.astype(BF16)
    rest = v - hi.astype(F32)
    mid = rest.astype(BF16)
    low = (rest - mid.astype(F32)).astype(BF16)
    return hi, mid, low


def row_norms(rows):
    square = jnp.square(rows.astype(F32))
    hi = square.astype(BF16)
    low = (square - hi.astype(F32)).astype(BF16)
    ones = jnp.ones((8, FEAT), BF16)
    return 0.5 * (dot(ones, hi, NT) + dot(ones, low, NT))[0:1, :]


def column_norms(rows):
    return 0.5 * jnp.sum(jnp.square(rows.astype(F32)), axis=1, keepdims=True)


def pack_pair(v):
    left = lax.broadcasted_iota(jnp.int32, (8, 128), 1) < CHUNK
    top, bottom = v[0:8], v[8:16]
    first = jnp.where(left, top, pltpu.roll(bottom, CHUNK, 1))
    second = jnp.where(left, pltpu.roll(top, CHUNK, 1), bottom)
    return first, second


def unpack_pair(a, b):
    left = lax.broadcasted_iota(jnp.int32, (8, 128), 1) < CHUNK
    top = jnp.where(left, a, pltpu.roll(b, CHUNK, 1))
    bottom = jnp.where(left, pltpu.roll(a, CHUNK, 1), b)
    return jnp.concatenate([top, bottom], axis=0)


def unpack(ref):
    wide = jnp.concatenate([unpack_pair(ref[2 * j], ref[2 * j + 1]) for j in range(GROUP // 2)], axis=1)
    return jnp.where(lax.broadcasted_iota(jnp.int32, wide.shape, 0) < 15, wide, 0.0)


def label_rows(labels):
    hi, mid, low = split3(labels)
    parts = [hi.astype(F32), mid.astype(F32), low.astype(F32), jnp.zeros((16, CHUNK), F32)]
    return jnp.concatenate(parts, axis=1).astype(BF16)


def labels_of(ref):
    left = lax.broadcasted_iota(jnp.int32, (16, 128), 1) < CHUNK
    whole = []
    for j in range(GROUP):
        block = ref[j, CHUNK:UNIT, :].astype(F32)
        a, b = block[:, 0:128], block[:, 128:256]
        whole.append((a + pltpu.roll(a, CHUNK, 1)) + (b + pltpu.roll(b, CHUNK, 1)))
    return jnp.concatenate([jnp.where(left, whole[2 * j], whole[2 * j + 1]) for j in range(GROUP // 2)], axis=1)


def gray(j):
    return j + (j // 2) * (5 - 2 * j)


def to_lanes(q, shift):
    sub = lax.broadcasted_iota(jnp.int32, (16, 128), 0)
    lane = lax.broadcasted_iota(jnp.int32, (16, 128), 1)
    return jnp.sum(jnp.where(lane == sub + shift, q, 0.0), axis=0, keepdims=True)


def from_lanes(row, shift):
    sub = lax.broadcasted_iota(jnp.int32, (16, 128), 0)
    lane = lax.broadcasted_iota(jnp.int32, (16, 128), 1)
    return jnp.sum(jnp.where(lane == sub + shift, row, 0.0), axis=1, keepdims=True)


def put_scalars(message, row):
    sub = lax.broadcasted_iota(jnp.int32, (8, 128), 0)
    lane = lax.broadcasted_iota(jnp.int32, (8, 128), 1)
    return jnp.where((sub == 7) & (lane >= CHUNK), row, message)


def lane_sum(v):
    return jnp.sum(v, axis=1, keepdims=True)


def ratio(a, b):
    real = lax.broadcasted_iota(jnp.int32, (16, 1), 0) < 15
    return jnp.where(real, a, 0.0) / jnp.where(real, b, 1.0)


def tree(values):
    values = list(values)
    while len(values) > 1:
        values = [values[i] + values[i + 1] if i + 1 < len(values) else values[i] for i in range(0, len(values), 2)]
    return values[0]


def kernel(
    sup_ref, lab_ref, tgt_hbm, tlab_hbm,
    coef_ref, grad_ref,
    tgt, tlab, unit, rf, cf, rows_all, rn_ref, sn_ref,
    kt_hi, kt_lo, kk_hi, kk_lo,
    s1_send, s1_recv, s2_send, s2_rows, s2_cols, s3_send, s3_recv,
    drow, rrow, xrow, dcol, rcol, prev,
    both, sib_send, sib_recv, pred_send, pred_recv, err_own, err, xt, gsum, csum, g_send, g_recv,
    local_sems, f_send, z_recv, x_recv, r_recv, b_recv, v_send, v_recv,
    sib_ss, sib_rs, pred_ss, pred_rs, err_ss, err_rs, g_ss, g_rs,
):
    r = lax.axis_index("row")
    c = lax.axis_index("col")
    chip, core = r // 2, lax.rem(r, 2)
    z, x = chip // 4, lax.rem(chip, 4)
    zl, y = c // 4, lax.rem(c, 4)
    me = core * 8 + c
    here = x * 4 + z

    def row_peer(j):
        k = lax.rem(core + j % 2, 2)
        p = lax.rem(zl + j // 8, 2) * 4 + lax.rem(y + gray((j // 2) % 4), 4)
        return k * 8 + p, (2 * chip + k, p)

    def chip_at(j):
        return lax.rem(z + gray(j // 4), 4), lax.rem(x + gray(j % 4), 4)

    def col_peer(j):
        pz, px = chip_at(j)
        return (2 * (pz * 4 + px) + core, c)

    def tile_at(j):
        pz, px = chip_at(j // 2)
        return 2 * (pz * 4 + px) + lax.rem(core + j % 2, 2)

    def far_first(count, act):
        @pl.loop(0, count - 1)
        def _(i):
            act(count - 1 - i)

    tgt_copy = pltpu.make_async_copy(tgt_hbm, tgt, local_sems.at[0])
    tgt_copy.start()
    start_lane = pl.multiple_of(r * TILE, TILE)
    tlab_copy = pltpu.make_async_copy(tlab_hbm.at[:, pl.ds(start_lane, TILE)], tlab, local_sems.at[1])
    tlab_copy.start()

    barrier = pltpu.get_barrier_semaphore()

    def greet_row(j):
        pl.semaphore_signal(barrier, inc=1, device_id=row_peer(j)[1], device_id_type=MESH)

    def greet_col(j):
        pl.semaphore_signal(barrier, inc=1, device_id=(tile_at(j), c), device_id_type=MESH)

    far_first(32, lambda j: pl.when(j > 1)(lambda: greet_col(j)))
    far_first(GROUP, greet_row)

    lab = jnp.concatenate([lab_ref[...], jnp.zeros((1, CHUNK), F32)], axis=0)
    unit[0:CHUNK, :] = sup_ref[...]
    unit[CHUNK:UNIT, :] = label_rows(lab)
    rf[me] = unit[...]
    cf[here] = unit[...]

    pl.semaphore_wait(barrier, 45)

    drains = []

    def remote(src, dst, ss, rs, to):
        return pltpu.make_async_remote_copy(
            src_ref=src, dst_ref=dst, send_sem=ss, recv_sem=rs, device_id=to, device_id_type=MESH
        )

    def wait_for(ref, sem):
        pltpu.make_async_copy(ref, ref, sem).wait()

    def device(pz, px):
        return (2 * (pz * 4 + px) + core, c)

    @pl.loop(0, 3)
    def _(i):
        to = device(lax.rem(z + gray(3 - i), 4), x)
        remote(unit, cf.at[here], f_send.at[0], z_recv.at[z], to).start()

    @pl.loop(0, 7)
    def _(i):
        j = 7 - i
        p = lax.rem(zl + j // 4, 2) * 4 + lax.rem(y + gray(j % 4), 4)
        remote(unit, rf.at[me], f_send.at[1], r_recv, (r, p)).start()

    def to_x(pz):
        @pl.loop(0, 3)
        def _(i):
            slot = x * 4 + pz
            remote(cf.at[slot], cf.at[slot], f_send.at[2], x_recv.at[x], device(z, lax.rem(x + gray(3 - i), 4))).start()

    to_x(z)

    @pl.loop(1, 4)
    def _(i):
        pz = lax.rem(z + gray(i), 4)
        wait_for(cf.at[0], z_recv.at[pz])
        to_x(pz)

    wait_for(rf.at[pl.ds(0, 7)], r_recv)
    block = pl.ds(core * 8, 8)
    other = 2 * chip + 1 - core
    remote(rf.at[block], rf.at[block], f_send.at[3], b_recv, (other, c)).start()
    drains.append((cf.at[pl.ds(0, 3)], f_send.at[0]))
    drains.append((rf.at[pl.ds(0, 7)], f_send.at[1]))
    drains.append((cf.at[pl.ds(0, 12)], f_send.at[2]))
    drains.append((rf.at[pl.ds(0, 8)], f_send.at[3]))

    half = pl.ds(pl.multiple_of(core * HALF, HALF), HALF)
    mine = rf[block][:, 0:CHUNK, :].reshape(HALF, FEAT)
    rows_all[half, :] = mine
    sn_ref[...] = column_norms(mine)
    tgt_copy.wait()

    def target_tile(i):
        rows = tgt[i]
        inner = dot(rows_all[half, :], rows, NT)
        value = jnp.exp(inner - sn_ref[...] - row_norms(rows))
        hi = value.astype(BF16)
        kk_hi[i] = hi
        kk_lo[i] = (value - hi.astype(F32)).astype(BF16)

    done = [0]

    def fill(count):
        stop = min(TILES, done[0] + count)
        if stop > done[0]:
            pl.loop(done[0], stop)(target_tile)
        done[0] = stop

    fill(10)

    wait_for(rf.at[pl.ds(0, 8)], b_recv)
    theirs = rf[pl.ds(8 - core * 8, 8)][:, 0:CHUNK, :].reshape(HALF, FEAT)
    rows_all[pl.ds(pl.multiple_of(HALF - core * HALF, HALF), HALF), :] = theirs
    rn_ref[...] = row_norms(rows_all[...])

    @pl.loop(0, 4)
    def _(i):
        px = lax.rem(x + gray(i), 4)

        @pl.when(i > 0)
        def _():
            wait_for(cf.at[pl.ds(0, 4)], x_recv.at[px])

        part = cf[pl.ds(px * 4, 4)][:, 0:CHUNK, :].reshape(TILE, FEAT)
        inner = dot(part, rows_all[...], NT)
        value = jnp.exp(inner - column_norms(part) - rn_ref[...])
        hi = value.astype(BF16)
        where = pl.ds(pl.multiple_of(px * TILE, TILE), TILE)
        kt_hi[where, :] = hi
        kt_lo[where, :] = (value - hi.astype(F32)).astype(BF16)

    def apply_tile(v):
        hi, mid, low = split3(v)
        big = dot(jnp.concatenate([hi, mid, low], axis=0), kt_hi[...])
        small = dot(jnp.concatenate([hi, mid], axis=0), kt_lo[...])
        return (big[0:16] + small[0:16]) + ((big[16:32] + small[16:32]) + big[32:48])

    b_rows = labels_of(rf)
    b_cols = labels_of(cf)
    drow[...] = b_rows
    rrow[...] = b_rows
    xrow[...] = jnp.zeros_like(b_rows)
    dcol[...] = b_cols
    rcol[...] = b_cols
    rr = None

    def predict_tiles(first, last):
        hi, mid, low = split3(xrow[:, half])
        hi2, mid2, low2 = split3(drow[:, half])
        three = jnp.concatenate([hi, hi2, mid, mid2, low, low2], axis=0)
        two = jnp.concatenate([hi, hi2, mid, mid2], axis=0)

        @pl.loop(first, last)
        def _(i):
            big = dot(three, kk_hi[i])
            small = dot(two, kk_lo[i])
            both[i] = (big[0:32] + small[0:32]) + ((big[32:64] + small[32:64]) + big[64:96])

    waits = ((5, 8), (5, 4))
    for step in range(3):
        last = step == 2
        applied = apply_tile(rcol[...])
        if step > 0:
            wait_for(s3_recv.at[step - 1, pl.ds(0, 15)], v_recv.at[step - 1, 3])
            new = from_lanes(tree([s3_recv[step - 1, j] for j in range(GROUP)])[7:8], CHUNK)
            beta = ratio(new, rr)
            rr = new
            applied = applied + beta * prev[...]
            drow[...] = rrow[...] + beta * drow[...]
            dcol[...] = rcol[...] + beta * dcol[...]
        prev[...] = applied
        d = drow[...]
        scalars = to_lanes(lane_sum(d * (applied + (RIDGE / GROUP) * d)), CHUNK)
        if step == 0:
            scalars = scalars + to_lanes(lane_sum(d * d) * (1.0 / GROUP), CHUNK + 16)
        if last:
            s1_send[step, 0] = put_scalars(jnp.zeros((8, 128), F32), scalars)
            s1_recv[step, me] = s1_send[step, 0]
        else:
            for j in range(GROUP // 2):
                first, second = pack_pair(applied[:, 128 * j:128 * (j + 1)])
                s1_send[step, 2 * j] = put_scalars(first, scalars)
                s1_send[step, 2 * j + 1] = put_scalars(second, scalars)
            s1_recv[step, me] = s1_send[step, me]

        def send1(j):
            p, to = row_peer(j)
            src = s1_send.at[step, 0] if last else s1_send.at[step, p]
            remote(src, s1_recv.at[step, me], v_send.at[step, 0], v_recv.at[step, 0], to).start()

        far_first(GROUP, send1)
        drains.append((s1_recv.at[step, pl.ds(0, 15)], v_send.at[step, 0]))
        if last:
            fill(TILES)
            predict_tiles(0, 12)
        else:
            fill(waits[step][0])
        wait_for(s1_recv.at[step, pl.ds(0, 15)], v_recv.at[step, 0])
        own = tree([s1_recv[step, j] for j in range(GROUP)])
        s2_send[step] = own
        s2_cols[step, here] = own

        def send2(j):
            remote(s2_send.at[step], s2_cols.at[step, here], v_send.at[step, 1], v_recv.at[step, 1], col_peer(j)).start()

        far_first(GROUP, send2)
        drains.append((s2_cols.at[step, pl.ds(0, 15)], v_send.at[step, 1]))
        if last:
            predict_tiles(12, TILES)
        else:
            s2_rows[step, me] = own

            def send_rows(j):
                remote(
                    s2_send.at[step], s2_rows.at[step, me], v_send.at[step, 2], v_recv.at[step, 2], row_peer(j)[1]
                ).start()

            far_first(GROUP, send_rows)
            drains.append((s2_rows.at[step, pl.ds(0, 15)], v_send.at[step, 2]))
            fill(waits[step][1])
        wait_for(s2_cols.at[step, pl.ds(0, 15)], v_recv.at[step, 1])
        total = tree([s2_cols[step, j] for j in range(GROUP)])[7:8]
        if step == 0:
            rr = from_lanes(total, CHUNK + 16)
        alpha = ratio(rr, from_lanes(total, CHUNK))
        if not last:
            left = rcol[...] - alpha * (unpack(s2_cols.at[step]) + RIDGE * dcol[...])
            rcol[...] = left
            s3_send[step] = put_scalars(jnp.zeros((8, 128), F32), to_lanes(lane_sum(left * left), CHUNK))
            s3_recv[step, me] = s3_send[step]

            def send3(j):
                remote(
                    s3_send.at[step], s3_recv.at[step, me], v_send.at[step, 3], v_recv.at[step, 3], row_peer(j)[1]
                ).start()

            far_first(GROUP, send3)
            drains.append((s3_recv.at[step, pl.ds(0, 15)], v_send.at[step, 3]))
            xrow[...] = xrow[...] + alpha * drow[...]
            wait_for(s2_rows.at[step, pl.ds(0, 15)], v_recv.at[step, 2])
            rrow[...] = rrow[...] - alpha * (unpack(s2_rows.at[step]) + RIDGE * drow[...])

    def combined(t):
        return both[t, 0:16, :] + alpha * both[t, 16:32, :]

    @pl.loop(0, 4)
    def _(g):
        quarter = pl.ds(12 - 4 * g, 4)
        for k in range(4):
            j = 12 - 4 * g + k
            sib_send[j] = combined(tile_at(2 * j + 1))
        remote(sib_send.at[quarter], sib_recv.at[quarter], sib_ss, sib_rs.at[3 - g], (other, c)).start()

    @pl.loop(0, 4)
    def _(g):
        wait_for(sib_recv.at[pl.ds(0, 4)], sib_rs.at[3 - g])
        for k in range(4):
            j = 15 - 4 * g - k
            t = tile_at(2 * j)
            value = combined(t) + sib_recv[j]

            @pl.when(j > 0)
            def _():
                pred_send[j] = value
                remote(pred_send.at[j], pred_recv.at[chip], pred_ss, pred_rs, (t, c)).start()

            @pl.when(j == 0)
            def _():
                pred_recv[chip] = value

    drains.append((sib_recv, sib_ss))
    drains.append((pred_recv.at[pl.ds(0, 15)], pred_ss))

    xrow[...] = xrow[...] + alpha * drow[...]
    pair = xrow[:, pl.ds(pl.multiple_of((me // 2) * 128, 128), 128)]
    own_x = jnp.where(lax.rem(me, 2) == 0, pair, pltpu.roll(pair, CHUNK, 1))
    coef_ref[...] = own_x[0:15, 0:CHUNK]
    hi, mid, low = split3(xrow[:, half])
    wide = jnp.concatenate([hi.astype(F32), mid.astype(F32), jnp.zeros((96, HALF), F32)], axis=0)
    xt[...] = wide.T[:, 0:32].astype(BF16)
    gsum[...] = jnp.zeros_like(gsum)
    csum[...] = jnp.zeros_like(csum)
    tlab_copy.wait()
    labels = jnp.concatenate([tlab[...], jnp.zeros((1, TILE), F32)], axis=0)

    wait_for(pred_recv.at[pl.ds(0, 15)], pred_rs)
    own_err = (tree([pred_recv[j] for j in range(GROUP)]) - labels).astype(BF16)
    err_own[...] = own_err
    err[r] = own_err

    def send_err(j):
        remote(err_own, err.at[r], err_ss, err_rs.at[r], (tile_at(j), c)).start()

    far_first(32, send_err)
    drains.append((err.at[pl.ds(0, 31)], err_ss))

    @pl.loop(0, 8)
    def _(s):
        part, sums = None, None
        for k in range(4):
            j = s * 4 + k
            t = tile_at(j)

            @pl.when(j > 0)
            def _():
                wait_for(err.at[0], err_rs.at[t])

            e = err[t]
            mix = dot(xt[...], jnp.concatenate([e, e], axis=0))
            weights = mix.astype(BF16) * kk_hi[t]
            product = dot(weights, tgt[t])
            back = weights.astype(F32)
            back = back[:, 0:128] + back[:, 128:256]
            part = product if part is None else part + product
            sums = back if sums is None else sums + back
        gsum[...] += part
        csum[...] += sums

    scale = 1.0 / 256.0
    term = (gsum[...] - lane_sum(csum[...]) * rows_all[half, :].astype(F32)) * scale
    g_send[...] = term.reshape(8, CHUNK, FEAT)
    g_recv[c] = g_send[c]

    @pl.loop(0, 7)
    def _(i):
        j = 7 - i
        p = lax.rem(zl + j // 4, 2) * 4 + lax.rem(y + gray(j % 4), 4)
        remote(g_send.at[p], g_recv.at[c], g_ss, g_rs, (r, p)).start()

    drains.append((g_recv.at[pl.ds(0, 7)], g_ss))
    wait_for(g_recv.at[pl.ds(0, 7)], g_rs)
    grad_ref[...] = tree([g_recv[j] for j in range(8)])

    for ref, sem in drains:
        wait_for(ref, sem)


def body(support, support_labels, targets, target_labels):
    classes = support_labels.shape[0]
    vmem = pl.BlockSpec(memory_space=pltpu.VMEM)
    anywhere = pl.BlockSpec(memory_space=pl.ANY)
    dma = pltpu.SemaphoreType.DMA
    return pl.pallas_call(
        kernel,
        out_shape=(
            jax.ShapeDtypeStruct((classes, CHUNK), F32),
            jax.ShapeDtypeStruct((CHUNK, FEAT), F32),
        ),
        in_specs=[vmem, vmem, anywhere, anywhere],
        out_specs=(vmem, vmem),
        scratch_shapes=[
            pltpu.VMEM((TILES, TILE, FEAT), BF16),
            pltpu.VMEM((classes, TILE), F32),
            pltpu.VMEM((UNIT, FEAT), BF16),
            pltpu.VMEM((GROUP, UNIT, FEAT), BF16),
            pltpu.VMEM((GROUP, UNIT, FEAT), BF16),
            pltpu.VMEM((WIDE, FEAT), BF16),
            pltpu.VMEM((1, WIDE), F32),
            pltpu.VMEM((HALF, 1), F32),
            pltpu.VMEM((WIDE, WIDE), BF16),
            pltpu.VMEM((WIDE, WIDE), BF16),
            pltpu.VMEM((TILES, HALF, TILE), BF16),
            pltpu.VMEM((TILES, HALF, TILE), BF16),
            pltpu.VMEM((3, GROUP, 8, 128), F32),
            pltpu.VMEM((3, GROUP, 8, 128), F32),
            pltpu.VMEM((3, 8, 128), F32),
            pltpu.VMEM((2, GROUP, 8, 128), F32),
            pltpu.VMEM((3, GROUP, 8, 128), F32),
            pltpu.VMEM((2, 8, 128), F32),
            pltpu.VMEM((2, GROUP, 8, 128), F32),
            pltpu.VMEM((GROUP, WIDE), F32),
            pltpu.VMEM((GROUP, WIDE), F32),
            pltpu.VMEM((GROUP, WIDE), F32),
            pltpu.VMEM((GROUP, WIDE), F32),
            pltpu.VMEM((GROUP, WIDE), F32),
            pltpu.VMEM((GROUP, WIDE), F32),
            pltpu.VMEM((TILES, 32, TILE), F32),
            pltpu.VMEM((GROUP, 16, TILE), F32),
            pltpu.VMEM((GROUP, 16, TILE), F32),
            pltpu.VMEM((GROUP, 16, TILE), F32),
            pltpu.VMEM((GROUP, 16, TILE), F32),
            pltpu.VMEM((16, TILE), BF16),
            pltpu.VMEM((TILES, 16, TILE), BF16),
            pltpu.VMEM((HALF, 32), BF16),
            pltpu.VMEM((HALF, FEAT), F32),
            pltpu.VMEM((HALF, 128), F32),
            pltpu.VMEM((8, CHUNK, FEAT), F32),
            pltpu.VMEM((8, CHUNK, FEAT), F32),
            dma((2,)),
            dma((4,)),
            dma((4,)),
            dma((4,)),
            dma,
            dma,
            dma((3, 4)),
            dma((3, 4)),
            dma,
            dma((4,)),
            dma,
            dma,
            dma,
            dma((TILES,)),
            dma,
            dma,
        ],
        compiler_params=pltpu.CompilerParams(
            collective_id=0, has_side_effects=True, vmem_limit_bytes=58 * 1024 * 1024
        ),
    )(support, support_labels, targets.reshape(TILES, TILE, FEAT), target_labels)


def solution(mesh):
    in_specs = (P(("row", "col"), None), P(None, ("row", "col")), P("col", None), P(None, "col"))
    out_specs = (P(None, ("row", "col")), P(("row", "col"), None))
    return jax.shard_map(body, mesh=mesh, in_specs=in_specs, out_specs=out_specs, check_vma=False)
```

time: 123 us -> 105 us (0.85)
  Pallas kernels: 119 us -> 102 us
    pallas_call x1, Pallas kernels: 119 us -> 102 us  [body(): pl.pallas_call(kernel, out_shape=(jax.ShapeDtypeStruct((classes, CHUNK),...]
where the time goes in v2:
time: 105 us
  Pallas kernels  102 us (97%)
  local copies, waits for them, and re-layouts  2.77 us (3%)
    pallas_call x1, Pallas kernels, body(): pl.pallas_call(kernel, out_shape=(jax.ShapeDtypeStruct((classes, CHUNK),...  102 us
    unnamed x2, local copies, waits for them, and re-layouts  2.77 us

profile of v2, /device:TPU:1, one launch (start us, length us, event | category | flops | bytes accessed | tf_op | source)
XLA Modules:
  0.0 105.2 jit_solution(16890302574658687848)
XLA Ops:
  0.6 101.8 %shard_map.59 = (f32[15,64]{1,0:T(8,128)}, f32[64,256]{1,0:T(8,128)}) custom-call(bf16[64,256]{1,0:T(8,128)(2,1)} %sup_ref.1, f32[15,64]{1,0:T(8,128)} %lab_ref.1, bf16[32,256,256]{2,1,0:T(8,128)(2,1)} %bitcast.1, f32[15,8192]{1,0:T(8,128)} %tlab_hbm.1), custom_call_target="tpu_custom_call" | custom-call | tf_op jit(solution)/shard_map/pallas_call | solution.py:491
  102.4 1.3 %copy.8 = f32[15,64]{1,0:T(8,128)} copy(f32[15,64]{1,0:T(8,128)} %get-tuple-element.4) | data formatting | bytes 7680
  103.7 1.5 %copy.9 = f32[64,256]{1,0:T(8,128)} copy(f32[64,256]{1,0:T(8,128)} %get-tuple-element.5) | data formatting | bytes 131072

commit v3 on v2

--- a/solution.py
+++ b/solution.py
@@ -122,10 +122,10 @@
 
 def kernel(
     sup_ref, lab_ref, tgt_hbm, tlab_hbm,
-    coef_ref, grad_ref,
+    out_ref,
     tgt, tlab, unit, rf, cf, rows_all, rn_ref, sn_ref,
     kt_hi, kt_lo, kk_hi, kk_lo,
-    s1_send, s1_recv, s2_send, s2_rows, s2_cols, s3_send, s3_recv,
+    s1_send, s1_recv, s2_send, s2_rows, s2_cols, s3_send, s3_recv, t_send, t_rows, t_cols,
     drow, rrow, xrow, dcol, rcol, prev,
     both, sib_send, sib_recv, pred_send, pred_recv, err_own, err, xt, gsum, csum, g_send, g_recv,
     local_sems, f_send, z_recv, x_recv, r_recv, b_recv, v_send, v_recv,
@@ -139,26 +139,30 @@
     me = core * 8 + c
     here = x * 4 + z
 
+    def device(pz, px):
+        return (2 * (pz * 4 + px) + core, c)
+
+    xs = [lax.rem(x + d, 4) for d in range(4)]
+    zs = [lax.rem(z + d, 4) for d in range(4)]
+    ys = [lax.rem(y + d, 4) for d in range(4)]
+    ls = [zl, 1 - zl]
+    ks = [core, 1 - core]
+
     def row_peer(j):
-        k = lax.rem(core + j % 2, 2)
-        p = lax.rem(zl + j // 8, 2) * 4 + lax.rem(y + gray((j // 2) % 4), 4)
+        k, p = ks[j % 2], ls[j // 8] * 4 + ys[gray((j // 2) % 4)]
         return k * 8 + p, (2 * chip + k, p)
 
-    def chip_at(j):
-        return lax.rem(z + gray(j // 4), 4), lax.rem(x + gray(j % 4), 4)
-
     def col_peer(j):
-        pz, px = chip_at(j)
-        return (2 * (pz * 4 + px) + core, c)
+        return (2 * (zs[gray(j // 4)] * 4 + xs[gray(j % 4)]) + core, c)
 
     def tile_at(j):
-        pz, px = chip_at(j // 2)
-        return 2 * (pz * 4 + px) + lax.rem(core + j % 2, 2)
+        j = jnp.int32(j)
+        chip_there = lax.rem(z + gray(j // 8), 4) * 4 + lax.rem(x + gray((j // 2) % 4), 4)
+        return 2 * chip_there + lax.rem(core + j % 2, 2)
 
     def far_first(count, act):
-        @pl.loop(0, count - 1)
-        def _(i):
-            act(count - 1 - i)
+        for j in range(count - 1, 0, -1):
+            act(j)
 
     tgt_copy = pltpu.make_async_copy(tgt_hbm, tgt, local_sems.at[0])
     tgt_copy.start()
@@ -167,15 +171,11 @@
     tlab_copy.start()
 
     barrier = pltpu.get_barrier_semaphore()
-
-    def greet_row(j):
-        pl.semaphore_signal(barrier, inc=1, device_id=row_peer(j)[1], device_id_type=MESH)
-
-    def greet_col(j):
-        pl.semaphore_signal(barrier, inc=1, device_id=(tile_at(j), c), device_id_type=MESH)
-
-    far_first(32, lambda j: pl.when(j > 1)(lambda: greet_col(j)))
-    far_first(GROUP, greet_row)
+    far_first(4, lambda j: pl.semaphore_signal(barrier, inc=1, device_id=device(zs[j], x), device_id_type=MESH))
+    far_first(4, lambda j: pl.semaphore_signal(barrier, inc=1, device_id=device(z, xs[j]), device_id_type=MESH))
+    far_first(
+        GROUP, lambda j: pl.semaphore_signal(barrier, inc=1, device_id=row_peer(j)[1], device_id_type=MESH)
+    )
 
     lab = jnp.concatenate([lab_ref[...], jnp.zeros((1, CHUNK), F32)], axis=0)
     unit[0:CHUNK, :] = sup_ref[...]
@@ -183,7 +183,7 @@
     rf[me] = unit[...]
     cf[here] = unit[...]
 
-    pl.semaphore_wait(barrier, 45)
+    pl.semaphore_wait(barrier, 21)
 
     drains = []
 
@@ -195,33 +195,22 @@
     def wait_for(ref, sem):
         pltpu.make_async_copy(ref, ref, sem).wait()
 
-    def device(pz, px):
-        return (2 * (pz * 4 + px) + core, c)
-
-    @pl.loop(0, 3)
-    def _(i):
-        to = device(lax.rem(z + gray(3 - i), 4), x)
-        remote(unit, cf.at[here], f_send.at[0], z_recv.at[z], to).start()
-
-    @pl.loop(0, 7)
-    def _(i):
-        j = 7 - i
-        p = lax.rem(zl + j // 4, 2) * 4 + lax.rem(y + gray(j % 4), 4)
-        remote(unit, rf.at[me], f_send.at[1], r_recv, (r, p)).start()
+    for d in (2, 3, 1):
+        remote(unit, cf.at[here], f_send.at[0], z_recv.at[z], device(zs[d], x)).start()
+    for j in range(7, 0, -1):
+        to = (r, ls[j // 4] * 4 + ys[gray(j % 4)])
+        remote(unit, rf.at[me], f_send.at[1], r_recv, to).start()
 
     def to_x(pz):
-        @pl.loop(0, 3)
-        def _(i):
+        for d in (2, 3, 1):
             slot = x * 4 + pz
-            remote(cf.at[slot], cf.at[slot], f_send.at[2], x_recv.at[x], device(z, lax.rem(x + gray(3 - i), 4))).start()
+            remote(cf.at[slot], cf.at[slot], f_send.at[2], x_recv.at[x], device(z, xs[d])).start()
 
     to_x(z)
 
-    @pl.loop(1, 4)
-    def _(i):
-        pz = lax.rem(z + gray(i), 4)
-        wait_for(cf.at[0], z_recv.at[pz])
-        to_x(pz)
+    for d in (1, 3, 2):
+        wait_for(cf.at[0], z_recv.at[zs[d]])
+        to_x(zs[d])
 
     wait_for(rf.at[pl.ds(0, 7)], r_recv)
     block = pl.ds(core * 8, 8)
@@ -292,17 +281,31 @@
     rcol[...] = b_cols
     rr = None
 
-    def predict_tiles(first, last):
+    def predict_tile(t):
         hi, mid, low = split3(xrow[:, half])
         hi2, mid2, low2 = split3(drow[:, half])
         three = jnp.concatenate([hi, hi2, mid, mid2, low, low2], axis=0)
         two = jnp.concatenate([hi, hi2, mid, mid2], axis=0)
-
-        @pl.loop(first, last)
-        def _(i):
-            big = dot(three, kk_hi[i])
-            small = dot(two, kk_lo[i])
-            both[i] = (big[0:32] + small[0:32]) + ((big[32:64] + small[32:64]) + big[64:96])
+        big = dot(three, kk_hi[t])
+        small = dot(two, kk_lo[t])
+        return (big[0:32] + small[0:32]) + ((big[32:64] + small[32:64]) + big[64:96])
+
+    def predict_theirs():
+        @pl.loop(0, 4)
+        def _(g):
+            for k in range(4):
+                j = 12 - 4 * g + k
+                sib_send[j] = predict_tile(tile_at(2 * j + 1))
+            quarter = pl.ds(12 - 4 * g, 4)
+            remote(sib_send.at[quarter], sib_recv.at[quarter], sib_ss, sib_rs.at[3 - g], (other, c)).start()
+
+    def predict_own():
+        @pl.loop(0, 4)
+        def _(g):
+            wait_for(sib_recv.at[pl.ds(0, 4)], sib_rs.at[3 - g])
+            for k in range(4):
+                j = 12 - 4 * g + k
+                both[j] = predict_tile(tile_at(2 * j)) + sib_recv[j]
 
     waits = ((5, 8), (5, 4))
     for step in range(3):
@@ -310,7 +313,7 @@
         applied = apply_tile(rcol[...])
         if step > 0:
             wait_for(s3_recv.at[step - 1, pl.ds(0, 15)], v_recv.at[step - 1, 3])
-            new = from_lanes(tree([s3_recv[step - 1, j] for j in range(GROUP)])[7:8], CHUNK)
+            new = from_lanes(tree([s3_recv[step - 1, j] for j in range(GROUP)]), CHUNK)
             beta = ratio(new, rr)
             rr = new
             applied = applied + beta * prev[...]
@@ -322,8 +325,8 @@
         if step == 0:
             scalars = scalars + to_lanes(lane_sum(d * d) * (1.0 / GROUP), CHUNK + 16)
         if last:
-            s1_send[step, 0] = put_scalars(jnp.zeros((8, 128), F32), scalars)
-            s1_recv[step, me] = s1_send[step, 0]
+            t_send[0] = scalars
+            t_rows[me] = scalars
         else:
             for j in range(GROUP // 2):
                 first, second = pack_pair(applied[:, 128 * j:128 * (j + 1)])
@@ -333,28 +336,38 @@
 
         def send1(j):
             p, to = row_peer(j)
-            src = s1_send.at[step, 0] if last else s1_send.at[step, p]
-            remote(src, s1_recv.at[step, me], v_send.at[step, 0], v_recv.at[step, 0], to).start()
+            src = t_send.at[0] if last else s1_send.at[step, p]
+            dst = t_rows.at[me] if last else s1_recv.at[step, me]
+            remote(src, dst, v_send.at[step, 0], v_recv.at[step, 0], to).start()
 
         far_first(GROUP, send1)
-        drains.append((s1_recv.at[step, pl.ds(0, 15)], v_send.at[step, 0]))
+        landed = t_rows.at[pl.ds(0, 15)] if last else s1_recv.at[step, pl.ds(0, 15)]
+        drains.append((landed, v_send.at[step, 0]))
         if last:
             fill(TILES)
-            predict_tiles(0, 12)
+            predict_theirs()
         else:
             fill(waits[step][0])
-        wait_for(s1_recv.at[step, pl.ds(0, 15)], v_recv.at[step, 0])
-        own = tree([s1_recv[step, j] for j in range(GROUP)])
-        s2_send[step] = own
-        s2_cols[step, here] = own
+        wait_for(landed, v_recv.at[step, 0])
+        if last:
+            own = tree([t_rows[j] for j in range(GROUP)])
+            t_send[1] = own
+            t_cols[here] = own
+        else:
+            own = tree([s1_recv[step, j] for j in range(GROUP)])
+            s2_send[step] = own
+            s2_cols[step, here] = own
 
         def send2(j):
-            remote(s2_send.at[step], s2_cols.at[step, here], v_send.at[step, 1], v_recv.at[step, 1], col_peer(j)).start()
+            src = t_send.at[1] if last else s2_send.at[step]
+            dst = t_cols.at[here] if last else s2_cols.at[step, here]
+            remote(src, dst, v_send.at[step, 1], v_recv.at[step, 1], col_peer(j)).start()
 
         far_first(GROUP, send2)
-        drains.append((s2_cols.at[step, pl.ds(0, 15)], v_send.at[step, 1]))
+        landed = t_cols.at[pl.ds(0, 15)] if last else s2_cols.at[step, pl.ds(0, 15)]
+        drains.append((landed, v_send.at[step, 1]))
         if last:
-            predict_tiles(12, TILES)
+            predict_own()
         else:
             s2_rows[step, me] = own
 
@@ -366,16 +379,20 @@
             far_first(GROUP, send_rows)
             drains.append((s2_rows.at[step, pl.ds(0, 15)], v_send.at[step, 2]))
             fill(waits[step][1])
-        wait_for(s2_cols.at[step, pl.ds(0, 15)], v_recv.at[step, 1])
-        total = tree([s2_cols[step, j] for j in range(GROUP)])[7:8]
+        wait_for(landed, v_recv.at[step, 1])
+        if last:
+            total = tree([t_cols[j] for j in range(GROUP)])
+        else:
+            total = tree([s2_cols[step, j] for j in range(GROUP)])[7:8]
         if step == 0:
             rr = from_lanes(total, CHUNK + 16)
         alpha = ratio(rr, from_lanes(total, CHUNK))
         if not last:
             left = rcol[...] - alpha * (unpack(s2_cols.at[step]) + RIDGE * dcol[...])
             rcol[...] = left
-            s3_send[step] = put_scalars(jnp.zeros((8, 128), F32), to_lanes(lane_sum(left * left), CHUNK))
-            s3_recv[step, me] = s3_send[step]
+            norms = to_lanes(lane_sum(left * left), CHUNK)
+            s3_send[step] = norms
+            s3_recv[step, me] = norms
 
             def send3(j):
                 remote(
@@ -388,33 +405,13 @@
             wait_for(s2_rows.at[step, pl.ds(0, 15)], v_recv.at[step, 2])
             rrow[...] = rrow[...] - alpha * (unpack(s2_rows.at[step]) + RIDGE * drow[...])
 
-    def combined(t):
-        return both[t, 0:16, :] + alpha * both[t, 16:32, :]
-
-    @pl.loop(0, 4)
-    def _(g):
-        quarter = pl.ds(12 - 4 * g, 4)
-        for k in range(4):
-            j = 12 - 4 * g + k
-            sib_send[j] = combined(tile_at(2 * j + 1))
-        remote(sib_send.at[quarter], sib_recv.at[quarter], sib_ss, sib_rs.at[3 - g], (other, c)).start()
-
-    @pl.loop(0, 4)
-    def _(g):
-        wait_for(sib_recv.at[pl.ds(0, 4)], sib_rs.at[3 - g])
-        for k in range(4):
-            j = 15 - 4 * g - k
-            t = tile_at(2 * j)
-            value = combined(t) + sib_recv[j]
-
-            @pl.when(j > 0)
-            def _():
-                pred_send[j] = value
-                remote(pred_send.at[j], pred_recv.at[chip], pred_ss, pred_rs, (t, c)).start()
-
-            @pl.when(j == 0)
-            def _():
-                pred_recv[chip] = value
+    for j in range(GROUP - 1, -1, -1):
+        value = both[j, 0:16, :] + alpha * both[j, 16:32, :]
+        if j > 0:
+            pred_send[j] = value
+            remote(pred_send.at[j], pred_recv.at[chip], pred_ss, pred_rs, col_peer(j)).start()
+        else:
+            pred_recv[chip] = value
 
     drains.append((sib_recv, sib_ss))
     drains.append((pred_recv.at[pl.ds(0, 15)], pred_ss))
@@ -422,7 +419,8 @@
     xrow[...] = xrow[...] + alpha * drow[...]
     pair = xrow[:, pl.ds(pl.multiple_of((me // 2) * 128, 128), 128)]
     own_x = jnp.where(lax.rem(me, 2) == 0, pair, pltpu.roll(pair, CHUNK, 1))
-    coef_ref[...] = own_x[0:15, 0:CHUNK]
+    out_ref[CHUNK:UNIT, 0:128] = own_x
+    out_ref[CHUNK:UNIT, 128:FEAT] = jnp.zeros((16, 128), F32)
     hi, mid, low = split3(xrow[:, half])
     wide = jnp.concatenate([hi.astype(F32), mid.astype(F32), jnp.zeros((96, HALF), F32)], axis=0)
     xt[...] = wide.T[:, 0:32].astype(BF16)
@@ -436,10 +434,10 @@
     err_own[...] = own_err
     err[r] = own_err
 
-    def send_err(j):
+    @pl.loop(1, 32)
+    def _(j):
         remote(err_own, err.at[r], err_ss, err_rs.at[r], (tile_at(j), c)).start()
 
-    far_first(32, send_err)
     drains.append((err.at[pl.ds(0, 31)], err_ss))
 
     @pl.loop(0, 8)
@@ -469,18 +467,21 @@
     g_send[...] = term.reshape(8, CHUNK, FEAT)
     g_recv[c] = g_send[c]
 
-    @pl.loop(0, 7)
-    def _(i):
-        j = 7 - i
-        p = lax.rem(zl + j // 4, 2) * 4 + lax.rem(y + gray(j % 4), 4)
+    for j in range(7, 0, -1):
+        p = ls[j // 4] * 4 + ys[gray(j % 4)]
         remote(g_send.at[p], g_recv.at[c], g_ss, g_rs, (r, p)).start()
 
     drains.append((g_recv.at[pl.ds(0, 7)], g_ss))
     wait_for(g_recv.at[pl.ds(0, 7)], g_rs)
-    grad_ref[...] = tree([g_recv[j] for j in range(8)])
+    out_ref[0:CHUNK, :] = tree([g_recv[j] for j in range(8)])
 
     for ref, sem in drains:
         wait_for(ref, sem)
+
+
+def part_outputs(joint_ref, coef_ref, grad_ref):
+    coef_ref[...] = joint_ref[CHUNK:CHUNK + 15, 0:CHUNK]
+    grad_ref[...] = joint_ref[0:CHUNK, :]
 
 
 def body(support, support_labels, targets, target_labels):
@@ -488,14 +489,11 @@
     vmem = pl.BlockSpec(memory_space=pltpu.VMEM)
     anywhere = pl.BlockSpec(memory_space=pl.ANY)
     dma = pltpu.SemaphoreType.DMA
-    return pl.pallas_call(
+    joint = pl.pallas_call(
         kernel,
-        out_shape=(
-            jax.ShapeDtypeStruct((classes, CHUNK), F32),
-            jax.ShapeDtypeStruct((CHUNK, FEAT), F32),
-        ),
+        out_shape=jax.ShapeDtypeStruct((UNIT, FEAT), F32),
         in_specs=[vmem, vmem, anywhere, anywhere],
-        out_specs=(vmem, vmem),
+        out_specs=vmem,
         scratch_shapes=[
             pltpu.VMEM((TILES, TILE, FEAT), BF16),
             pltpu.VMEM((classes, TILE), F32),
@@ -509,22 +507,25 @@
             pltpu.VMEM((WIDE, WIDE), BF16),
             pltpu.VMEM((TILES, HALF, TILE), BF16),
             pltpu.VMEM((TILES, HALF, TILE), BF16),
-            pltpu.VMEM((3, GROUP, 8, 128), F32),
-            pltpu.VMEM((3, GROUP, 8, 128), F32),
-            pltpu.VMEM((3, 8, 128), F32),
             pltpu.VMEM((2, GROUP, 8, 128), F32),
-            pltpu.VMEM((3, GROUP, 8, 128), F32),
+            pltpu.VMEM((2, GROUP, 8, 128), F32),
             pltpu.VMEM((2, 8, 128), F32),
             pltpu.VMEM((2, GROUP, 8, 128), F32),
+            pltpu.VMEM((2, GROUP, 8, 128), F32),
+            pltpu.VMEM((2, 1, 128), F32),
+            pltpu.VMEM((2, GROUP, 1, 128), F32),
+            pltpu.VMEM((2, 1, 128), F32),
+            pltpu.VMEM((GROUP, 1, 128), F32),
+            pltpu.VMEM((GROUP, 1, 128), F32),
             pltpu.VMEM((GROUP, WIDE), F32),
             pltpu.VMEM((GROUP, WIDE), F32),
             pltpu.VMEM((GROUP, WIDE), F32),
             pltpu.VMEM((GROUP, WIDE), F32),
             pltpu.VMEM((GROUP, WIDE), F32),
             pltpu.VMEM((GROUP, WIDE), F32),
-            pltpu.VMEM((TILES, 32, TILE), F32),
-            pltpu.VMEM((GROUP, 16, TILE), F32),
-            pltpu.VMEM((GROUP, 16, TILE), F32),
+            pltpu.VMEM((GROUP, 32, TILE), F32),
+            pltpu.VMEM((GROUP, 32, TILE), F32),
+            pltpu.VMEM((GROUP, 32, TILE), F32),
             pltpu.VMEM((GROUP, 16, TILE), F32),
             pltpu.VMEM((GROUP, 16, TILE), F32),
             pltpu.VMEM((16, TILE), BF16),
@@ -555,6 +556,15 @@
             collective_id=0, has_side_effects=True, vmem_limit_bytes=58 * 1024 * 1024
         ),
     )(support, support_labels, targets.reshape(TILES, TILE, FEAT), target_labels)
+    return pl.pallas_call(
+        part_outputs,
+        out_shape=(
+            jax.ShapeDtypeStruct((classes, CHUNK), F32),
+            jax.ShapeDtypeStruct((CHUNK, FEAT), F32),
+        ),
+        in_specs=[vmem],
+        out_specs=(vmem, vmem),
+    )(joint)
 
 
 def solution(mesh):

time: 105 us -> 98.6 us (0.939)
  Pallas kernels: 102 us -> 97.8 us
  local copies, waits for them, and re-layouts: 2.77 us -> 0 us
    pallas_call x1 -> x2, Pallas kernels: 102 us -> 97.8 us  [the longest x1 96.3 us: body(): pl.pallas_call(kernel, out_shape=jax.ShapeDtypeStruct((UNIT, FEAT), F32),...]
    unnamed x2 -> x0, local copies, waits for them, and re-layouts: 2.77 us -> none
where the time goes in v3:
time: 98.6 us; the launch traced here: 98.4 us
  Pallas kernels  97.8 us (99%)
    pallas_call x1, Pallas kernels, body(): pl.pallas_call(kernel, out_shape=jax.ShapeDtypeStruct((UNIT, FEAT), F32),...  96.3 us

profile of v3, /device:TPU:1, one launch (start us, length us, event | category | flops | bytes accessed | tf_op | source)
XLA Modules:
  0.0 98.4 jit_solution(16973161666660773934)
XLA Ops:
  0.6 96.3 %shard_map.59.joint_ref = f32[80,256]{1,0:T(8,128)} custom-call(bf16[64,256]{1,0:T(8,128)(2,1)} %sup_ref.1, f32[15,64]{1,0:T(8,128)} %lab_ref.1, bf16[32,256,256]{2,1,0:T(8,128)(2,1)} %bitcast.1, f32[15,8192]{1,0:T(8,128)} %tlab_hbm.1), custom_call_target="tpu_custom_call" | custom-call | tf_op jit(solution)/shard_map/pallas_call | solution.py:492
  96.9 1.5 %shard_map.60 = (f32[15,64]{1,0:T(8,128)}, f32[64,256]{1,0:T(8,128)}) custom-call(f32[80,256]{1,0:T(8,128)} %shard_map.59.joint_ref), custom_call_target="tpu_custom_call" | custom-call | tf_op jit(solution)/shard_map/pallas_call | solution.py:559

commit v4 on v3

--- a/solution.py
+++ b/solution.py
@@ -17,7 +17,6 @@
 WIDE = GROUP * CHUNK
 HALF = WIDE // 2
 RIDGE = 0.5
-UNIT = CHUNK + 16
 NN = (((1,), (0,)), ((), ()))
 NT = (((1,), (1,)), ((), ()))
 
@@ -66,22 +65,6 @@
     return jnp.where(lax.broadcasted_iota(jnp.int32, wide.shape, 0) < 15, wide, 0.0)
 
 
-def label_rows(labels):
-    hi, mid, low = split3(labels)
-    parts = [hi.astype(F32), mid.astype(F32), low.astype(F32), jnp.zeros((16, CHUNK), F32)]
-    return jnp.concatenate(parts, axis=1).astype(BF16)
-
-
-def labels_of(ref):
-    left = lax.broadcasted_iota(jnp.int32, (16, 128), 1) < CHUNK
-    whole = []
-    for j in range(GROUP):
-        block = ref[j, CHUNK:UNIT, :].astype(F32)
-        a, b = block[:, 0:128], block[:, 128:256]
-        whole.append((a + pltpu.roll(a, CHUNK, 1)) + (b + pltpu.roll(b, CHUNK, 1)))
-    return jnp.concatenate([jnp.where(left, whole[2 * j], whole[2 * j + 1]) for j in range(GROUP // 2)], axis=1)
-
-
 def gray(j):
     return j + (j // 2) * (5 - 2 * j)
 
@@ -123,13 +106,13 @@
 def kernel(
     sup_ref, lab_ref, tgt_hbm, tlab_hbm,
     out_ref,
-    tgt, tlab, unit, rf, cf, rows_all, rn_ref, sn_ref,
+    tgt, tlab, sup_v, lab_v, rf, cf, lab_rows, lab_cols, rn_ref, sn_ref,
     kt_hi, kt_lo, kk_hi, kk_lo,
-    s1_send, s1_recv, s2_send, s2_rows, s2_cols, s3_send, s3_recv, t_send, t_rows, t_cols,
+    s1_send, s1_recv, s2_send, s2_rows, s2_cols, t_send, t_rows, t_cols,
     drow, rrow, xrow, dcol, rcol, prev,
-    both, sib_send, sib_recv, pred_send, pred_recv, err_own, err, xt, gsum, csum, g_send, g_recv,
-    local_sems, f_send, z_recv, x_recv, r_recv, b_recv, v_send, v_recv,
-    sib_ss, sib_rs, pred_ss, pred_rs, err_ss, err_rs, g_ss, g_rs,
+    three, both, sib_send, sib_recv, pred_send, pred_recv, err_own, err, xt, gsum, csum, g_send, g_recv,
+    local_sems, f_send, z_recv, x_recv, r_recv, l_send, l_recv, v_send, v_recv,
+    sib_ss, sib_rs, pred_ss, pred_rs, err_ss, err_rs, pass_ss, g_ss, g_rs,
 ):
     r = lax.axis_index("row")
     c = lax.axis_index("col")
@@ -178,10 +161,13 @@
     )
 
     lab = jnp.concatenate([lab_ref[...], jnp.zeros((1, CHUNK), F32)], axis=0)
-    unit[0:CHUNK, :] = sup_ref[...]
-    unit[CHUNK:UNIT, :] = label_rows(lab)
-    rf[me] = unit[...]
-    cf[here] = unit[...]
+    lab_v[...] = jnp.concatenate([lab[0:8], lab[8:16]], axis=1)
+    sup = sup_ref[...]
+    sup_v[...] = sup
+    rf[me] = sup
+    cf[here] = sup
+    lab_rows[me] = lab_v[...]
+    lab_cols[here] = lab_v[...]
 
     pl.semaphore_wait(barrier, 21)
 
@@ -195,41 +181,65 @@
     def wait_for(ref, sem):
         pltpu.make_async_copy(ref, ref, sem).wait()
 
+    def to_x(dz, steps):
+        slot = xs[0] * 4 + zs[dz]
+        for d in steps:
+            remote(cf.at[slot], cf.at[slot], f_send.at[2], x_recv.at[slot], device(z, xs[d])).start()
+
+    def from_x(dx, dz):
+        slot = xs[dx] * 4 + zs[dz]
+        wait_for(cf.at[0], x_recv.at[slot])
+        return slot
+
+    def pass_on(dx, dz):
+        slot = from_x(dx, dz)
+        remote(cf.at[slot], cf.at[slot], f_send.at[2], x_recv.at[slot], device(z, xs[4 - dx])).start()
+
+    col_peers = [(r, ls[j // 4] * 4 + ys[gray(j % 4)]) for j in range(8)]
     for d in (2, 3, 1):
-        remote(unit, cf.at[here], f_send.at[0], z_recv.at[z], device(zs[d], x)).start()
+        remote(sup_v, cf.at[here], f_send.at[0], z_recv.at[z], device(zs[d], x)).start()
+    to_x(0, (1, 3))
     for j in range(7, 0, -1):
-        to = (r, ls[j // 4] * 4 + ys[gray(j % 4)])
-        remote(unit, rf.at[me], f_send.at[1], r_recv, to).start()
-
-    def to_x(pz):
-        for d in (2, 3, 1):
-            slot = x * 4 + pz
-            remote(cf.at[slot], cf.at[slot], f_send.at[2], x_recv.at[x], device(z, xs[d])).start()
-
-    to_x(z)
-
-    for d in (1, 3, 2):
+        remote(sup_v, rf.at[me], f_send.at[1], r_recv.at[0], col_peers[j]).start()
+    for d in (2, 3, 1):
+        remote(lab_v, lab_cols.at[here], l_send.at[0], l_recv.at[0], device(zs[d], x)).start()
+    for j in range(7, 0, -1):
+        remote(lab_v, lab_rows.at[me], l_send.at[1], l_recv.at[1], col_peers[j]).start()
+
+    for d in (1, 3):
         wait_for(cf.at[0], z_recv.at[zs[d]])
-        to_x(zs[d])
-
-    wait_for(rf.at[pl.ds(0, 7)], r_recv)
+        to_x(d, (1, 3))
+    pass_on(1, 0)
+    wait_for(cf.at[0], z_recv.at[zs[2]])
+    to_x(2, (1, 3))
+
     block = pl.ds(core * 8, 8)
     other = 2 * chip + 1 - core
-    remote(rf.at[block], rf.at[block], f_send.at[3], b_recv, (other, c)).start()
+    wait_for(rf.at[pl.ds(0, 7)], r_recv.at[0])
+    remote(rf.at[block], rf.at[block], f_send.at[3], r_recv.at[1], (other, c)).start()
+    wait_for(lab_cols.at[pl.ds(0, 3)], l_recv.at[0])
+    for d in (2, 3, 1):
+        four = lab_cols.at[pl.ds(x * 4, 4)]
+        remote(four, four, l_send.at[2], l_recv.at[2], device(z, xs[d])).start()
+    wait_for(lab_rows.at[pl.ds(0, 7)], l_recv.at[1])
+    remote(lab_rows.at[block], lab_rows.at[block], l_send.at[3], l_recv.at[3], (other, c)).start()
+
     drains.append((cf.at[pl.ds(0, 3)], f_send.at[0]))
     drains.append((rf.at[pl.ds(0, 7)], f_send.at[1]))
     drains.append((cf.at[pl.ds(0, 12)], f_send.at[2]))
     drains.append((rf.at[pl.ds(0, 8)], f_send.at[3]))
+    drains.append((lab_cols.at[pl.ds(0, 3)], l_send.at[0]))
+    drains.append((lab_rows.at[pl.ds(0, 7)], l_send.at[1]))
+    drains.append((lab_cols.at[pl.ds(0, 12)], l_send.at[2]))
+    drains.append((lab_rows.at[pl.ds(0, 8)], l_send.at[3]))
 
     half = pl.ds(pl.multiple_of(core * HALF, HALF), HALF)
-    mine = rf[block][:, 0:CHUNK, :].reshape(HALF, FEAT)
-    rows_all[half, :] = mine
-    sn_ref[...] = column_norms(mine)
+    sn_ref[...] = column_norms(rf[block].reshape(HALF, FEAT))
     tgt_copy.wait()
 
     def target_tile(i):
         rows = tgt[i]
-        inner = dot(rows_all[half, :], rows, NT)
+        inner = dot(rf[block].reshape(HALF, FEAT), rows, NT)
         value = jnp.exp(inner - sn_ref[...] - row_norms(rows))
         hi = value.astype(BF16)
         kk_hi[i] = hi
@@ -240,26 +250,43 @@
     def fill(count):
         stop = min(TILES, done[0] + count)
         if stop > done[0]:
-            pl.loop(done[0], stop)(target_tile)
+
+            @pl.loop(done[0] // 2, stop // 2)
+            def _(i):
+                target_tile(2 * i)
+                target_tile(2 * i + 1)
+
         done[0] = stop
 
-    fill(10)
-
-    wait_for(rf.at[pl.ds(0, 8)], b_recv)
-    theirs = rf[pl.ds(8 - core * 8, 8)][:, 0:CHUNK, :].reshape(HALF, FEAT)
-    rows_all[pl.ds(pl.multiple_of(HALF - core * HALF, HALF), HALF), :] = theirs
-    rn_ref[...] = row_norms(rows_all[...])
+    fill(4)
+    pass_on(3, 1)
+    pass_on(3, 3)
+    pass_on(1, 2)
+    fill(4)
+
+    wait_for(rf.at[pl.ds(0, 8)], r_recv.at[1])
+    rn_ref[...] = row_norms(rf[...].reshape(WIDE, FEAT))
 
     @pl.loop(0, 4)
     def _(i):
+        @pl.when(i == 1)
+        def _():
+            from_x(1, 1)
+            from_x(1, 3)
+
+        @pl.when(i == 2)
+        def _():
+            from_x(3, 0)
+            from_x(3, 2)
+
+        @pl.when(i == 3)
+        def _():
+            for d in range(4):
+                from_x(2, d)
+
         px = lax.rem(x + gray(i), 4)
-
-        @pl.when(i > 0)
-        def _():
-            wait_for(cf.at[pl.ds(0, 4)], x_recv.at[px])
-
-        part = cf[pl.ds(px * 4, 4)][:, 0:CHUNK, :].reshape(TILE, FEAT)
-        inner = dot(part, rows_all[...], NT)
+        part = cf[pl.ds(px * 4, 4)].reshape(TILE, FEAT)
+        inner = dot(part, rf[...].reshape(WIDE, FEAT), NT)
         value = jnp.exp(inner - column_norms(part) - rn_ref[...])
         hi = value.astype(BF16)
         where = pl.ds(pl.multiple_of(px * TILE, TILE), TILE)
@@ -272,8 +299,10 @@
         small = dot(jnp.concatenate([hi, mid], axis=0), kt_lo[...])
         return (big[0:16] + small[0:16]) + ((big[16:32] + small[16:32]) + big[32:48])
 
-    b_rows = labels_of(rf)
-    b_cols = labels_of(cf)
+    wait_for(lab_cols.at[pl.ds(0, 12)], l_recv.at[2])
+    b_cols = unpack(lab_cols)
+    wait_for(lab_rows.at[pl.ds(0, 8)], l_recv.at[3])
+    b_rows = unpack(lab_rows)
     drow[...] = b_rows
     rrow[...] = b_rows
     xrow[...] = jnp.zeros_like(b_rows)
@@ -282,12 +311,8 @@
     rr = None
 
     def predict_tile(t):
-        hi, mid, low = split3(xrow[:, half])
-        hi2, mid2, low2 = split3(drow[:, half])
-        three = jnp.concatenate([hi, hi2, mid, mid2, low, low2], axis=0)
-        two = jnp.concatenate([hi, hi2, mid, mid2], axis=0)
-        big = dot(three, kk_hi[t])
-        small = dot(two, kk_lo[t])
+        big = dot(three[...], kk_hi[t])
+        small = dot(three[0:64, :], kk_lo[t])
         return (big[0:32] + small[0:32]) + ((big[32:64] + small[32:64]) + big[64:96])
 
     def predict_theirs():
@@ -307,31 +332,35 @@
                 j = 12 - 4 * g + k
                 both[j] = predict_tile(tile_at(2 * j)) + sib_recv[j]
 
-    waits = ((5, 8), (5, 4))
+    lane = lax.broadcasted_iota(jnp.int32, (1, 128), 1)
+    left_half = lax.broadcasted_iota(jnp.int32, (8, 128), 1) < CHUNK
+    waits = ((8, 8), (4, 4))
     for step in range(3):
-        last = step == 2
+        first, last = step == 0, step == 2
+        norm = lane_sum(rcol[...] * rcol[...])
         applied = apply_tile(rcol[...])
-        if step > 0:
-            wait_for(s3_recv.at[step - 1, pl.ds(0, 15)], v_recv.at[step - 1, 3])
-            new = from_lanes(tree([s3_recv[step - 1, j] for j in range(GROUP)]), CHUNK)
-            beta = ratio(new, rr)
-            rr = new
-            applied = applied + beta * prev[...]
-            drow[...] = rrow[...] + beta * drow[...]
-            dcol[...] = rcol[...] + beta * dcol[...]
-        prev[...] = applied
-        d = drow[...]
-        scalars = to_lanes(lane_sum(d * (applied + (RIDGE / GROUP) * d)), CHUNK)
-        if step == 0:
-            scalars = scalars + to_lanes(lane_sum(d * d) * (1.0 / GROUP), CHUNK + 16)
+        small_ridge = RIDGE / GROUP
+        if first:
+            d = drow[...]
+            guess = applied
+            scalars = to_lanes(lane_sum(d * (applied + small_ridge * d)), CHUNK) + to_lanes(norm, CHUNK + 48)
+        else:
+            near = ratio(norm * float(GROUP), rr)
+            old = drow[...]
+            d = rrow[...] + near * old
+            guess = applied + near * prev[...]
+            by_d = guess + small_ridge * d
+            by_old = prev[...] + small_ridge * old
+            scalars = to_lanes(lane_sum(d * by_d), CHUNK) + to_lanes(lane_sum(d * by_old + old * by_d), CHUNK + 16)
+            scalars = scalars + to_lanes(lane_sum(old * by_old), CHUNK + 32) + to_lanes(norm, CHUNK + 48)
         if last:
             t_send[0] = scalars
             t_rows[me] = scalars
         else:
             for j in range(GROUP // 2):
-                first, second = pack_pair(applied[:, 128 * j:128 * (j + 1)])
-                s1_send[step, 2 * j] = put_scalars(first, scalars)
-                s1_send[step, 2 * j + 1] = put_scalars(second, scalars)
+                a, b = pack_pair(applied[:, 128 * j:128 * (j + 1)])
+                s1_send[step, 2 * j] = put_scalars(a, scalars)
+                s1_send[step, 2 * j + 1] = put_scalars(b, scalars)
             s1_recv[step, me] = s1_send[step, me]
 
         def send1(j):
@@ -345,16 +374,37 @@
         drains.append((landed, v_send.at[step, 0]))
         if last:
             fill(TILES)
-            predict_theirs()
         else:
             fill(waits[step][0])
         wait_for(landed, v_recv.at[step, 0])
         if last:
-            own = tree([t_rows[j] for j in range(GROUP)])
-            t_send[1] = own
-            t_cols[here] = own
+            scalar_rows = [t_rows[j] for j in range(GROUP)]
+        else:
+            scalar_rows = [s1_recv[step, j][7:8] for j in range(GROUP)]
+        sums = tree(scalar_rows)
+        if first:
+            rr = from_lanes(sums, CHUNK + 48)
+            share = sums
+        else:
+            held = (lane >= CHUNK + 48) & (lane < CHUNK + 63)
+            under = jnp.where(held, to_lanes(rr, CHUNK + 48), 1.0)
+            senders = jnp.concatenate(scalar_rows, axis=0)
+            true = jnp.where(held, sums, 0.0) / under
+            off = true - jnp.where(held, senders * float(GROUP), 0.0) / under
+            off = pltpu.roll(off, 80, 1)
+            share = senders + off * (pltpu.roll(senders, 112, 1) + off * pltpu.roll(senders, 96, 1))
+            share = jnp.sum(share, axis=0, keepdims=True)
+            new = from_lanes(sums, CHUNK + 48)
+            beta = ratio(new, rr)
+            rr = new
+        if last:
+            t_send[1] = share
+            t_cols[here] = share
         else:
             own = tree([s1_recv[step, j] for j in range(GROUP)])
+            if not first:
+                own = own + jnp.where(left_half, beta[0:8], beta[8:16]) * s2_send[step - 1]
+            own = put_scalars(own, share)
             s2_send[step] = own
             s2_cols[step, here] = own
 
@@ -366,9 +416,7 @@
         far_first(GROUP, send2)
         landed = t_cols.at[pl.ds(0, 15)] if last else s2_cols.at[step, pl.ds(0, 15)]
         drains.append((landed, v_send.at[step, 1]))
-        if last:
-            predict_own()
-        else:
+        if not last:
             s2_rows[step, me] = own
 
             def send_rows(j):
@@ -378,29 +426,29 @@
 
             far_first(GROUP, send_rows)
             drains.append((s2_rows.at[step, pl.ds(0, 15)], v_send.at[step, 2]))
+        if first:
+            prev[...] = applied
+        else:
+            drow[...] = rrow[...] + beta * drow[...]
+            if not last:
+                prev[...] = applied + beta * prev[...]
+                dcol[...] = rcol[...] + beta * dcol[...]
+        if last:
+            hi, mid, low = split3(xrow[:, half])
+            hi2, mid2, low2 = split3(drow[:, half])
+            three[...] = jnp.concatenate([hi, hi2, mid, mid2, low, low2], axis=0)
+            predict_theirs()
+            predict_own()
+        else:
             fill(waits[step][1])
         wait_for(landed, v_recv.at[step, 1])
         if last:
             total = tree([t_cols[j] for j in range(GROUP)])
         else:
-            total = tree([s2_cols[step, j] for j in range(GROUP)])[7:8]
-        if step == 0:
-            rr = from_lanes(total, CHUNK + 16)
+            total = tree([s2_cols[step, j][7:8] for j in range(GROUP)])
         alpha = ratio(rr, from_lanes(total, CHUNK))
         if not last:
-            left = rcol[...] - alpha * (unpack(s2_cols.at[step]) + RIDGE * dcol[...])
-            rcol[...] = left
-            norms = to_lanes(lane_sum(left * left), CHUNK)
-            s3_send[step] = norms
-            s3_recv[step, me] = norms
-
-            def send3(j):
-                remote(
-                    s3_send.at[step], s3_recv.at[step, me], v_send.at[step, 3], v_recv.at[step, 3], row_peer(j)[1]
-                ).start()
-
-            far_first(GROUP, send3)
-            drains.append((s3_recv.at[step, pl.ds(0, 15)], v_send.at[step, 3]))
+            rcol[...] = rcol[...] - alpha * (unpack(s2_cols.at[step]) + RIDGE * dcol[...])
             xrow[...] = xrow[...] + alpha * drow[...]
             wait_for(s2_rows.at[step, pl.ds(0, 15)], v_recv.at[step, 2])
             rrow[...] = rrow[...] - alpha * (unpack(s2_rows.at[step]) + RIDGE * drow[...])
@@ -419,8 +467,8 @@
     xrow[...] = xrow[...] + alpha * drow[...]
     pair = xrow[:, pl.ds(pl.multiple_of((me // 2) * 128, 128), 128)]
     own_x = jnp.where(lax.rem(me, 2) == 0, pair, pltpu.roll(pair, CHUNK, 1))
-    out_ref[CHUNK:UNIT, 0:128] = own_x
-    out_ref[CHUNK:UNIT, 128:FEAT] = jnp.zeros((16, 128), F32)
+    out_ref[CHUNK:CHUNK + 16, 0:128] = own_x
+    out_ref[CHUNK:CHUNK + 16, 128:FEAT] = jnp.zeros((16, 128), F32)
     hi, mid, low = split3(xrow[:, half])
     wide = jnp.concatenate([hi.astype(F32), mid.astype(F32), jnp.zeros((96, HALF), F32)], axis=0)
     xt[...] = wide.T[:, 0:32].astype(BF16)
@@ -434,23 +482,13 @@
     err_own[...] = own_err
     err[r] = own_err
 
-    @pl.loop(1, 32)
-    def _(j):
-        remote(err_own, err.at[r], err_ss, err_rs.at[r], (tile_at(j), c)).start()
-
-    drains.append((err.at[pl.ds(0, 31)], err_ss))
-
-    @pl.loop(0, 8)
-    def _(s):
+    for j in range(1, GROUP):
+        remote(err_own, err.at[r], err_ss, err_rs.at[r], col_peer(j)).start()
+    drains.append((err.at[pl.ds(0, 15)], err_ss))
+
+    def add_tiles(tiles):
         part, sums = None, None
-        for k in range(4):
-            j = s * 4 + k
-            t = tile_at(j)
-
-            @pl.when(j > 0)
-            def _():
-                wait_for(err.at[0], err_rs.at[t])
-
+        for t in tiles:
             e = err[t]
             mix = dot(xt[...], jnp.concatenate([e, e], axis=0))
             weights = mix.astype(BF16) * kk_hi[t]
@@ -462,14 +500,39 @@
         gsum[...] += part
         csum[...] += sums
 
+    def take_own(j):
+        t = tile_at(2 * j)
+
+        @pl.when(j > 0)
+        def _():
+            wait_for(err.at[0], err_rs.at[t])
+
+        remote(err.at[t], err.at[t], pass_ss, err_rs.at[t], (other, c)).start()
+        return t
+
+    def take_theirs(j):
+        t = tile_at(2 * j + 1)
+        wait_for(err.at[0], err_rs.at[t])
+        return t
+
+    zero = jnp.int32(0)
+    add_tiles([take_own(zero), take_own(zero + 1)])
+
+    @pl.loop(1, 8)
+    def _(s):
+        mine = [take_own(2 * s), take_own(2 * s + 1)]
+        add_tiles([take_theirs(2 * s - 2), take_theirs(2 * s - 1)] + mine)
+
+    add_tiles([take_theirs(zero + 14), take_theirs(zero + 15)])
+    drains.append((err.at[pl.ds(0, 16)], pass_ss))
+
     scale = 1.0 / 256.0
-    term = (gsum[...] - lane_sum(csum[...]) * rows_all[half, :].astype(F32)) * scale
+    term = (gsum[...] - lane_sum(csum[...]) * rf[block].reshape(HALF, FEAT).astype(F32)) * scale
     g_send[...] = term.reshape(8, CHUNK, FEAT)
     g_recv[c] = g_send[c]
 
     for j in range(7, 0, -1):
-        p = ls[j // 4] * 4 + ys[gray(j % 4)]
-        remote(g_send.at[p], g_recv.at[c], g_ss, g_rs, (r, p)).start()
+        remote(g_send.at[col_peers[j][1]], g_recv.at[c], g_ss, g_rs, col_peers[j]).start()
 
     drains.append((g_recv.at[pl.ds(0, 7)], g_ss))
     wait_for(g_recv.at[pl.ds(0, 7)], g_rs)
@@ -491,16 +554,18 @@
     dma = pltpu.SemaphoreType.DMA
     joint = pl.pallas_call(
         kernel,
-        out_shape=jax.ShapeDtypeStruct((UNIT, FEAT), F32),
+        out_shape=jax.ShapeDtypeStruct((CHUNK + 16, FEAT), F32),
         in_specs=[vmem, vmem, anywhere, anywhere],
         out_specs=vmem,
         scratch_shapes=[
             pltpu.VMEM((TILES, TILE, FEAT), BF16),
             pltpu.VMEM((classes, TILE), F32),
-            pltpu.VMEM((UNIT, FEAT), BF16),
-            pltpu.VMEM((GROUP, UNIT, FEAT), BF16),
-            pltpu.VMEM((GROUP, UNIT, FEAT), BF16),
-            pltpu.VMEM((WIDE, FEAT), BF16),
+            pltpu.VMEM((CHUNK, FEAT), BF16),
+            pltpu.VMEM((8, 128), F32),
+            pltpu.VMEM((GROUP, CHUNK, FEAT), BF16),
+            pltpu.VMEM((GROUP, CHUNK, FEAT), BF16),
+            pltpu.VMEM((GROUP, 8, 128), F32),
+            pltpu.VMEM((GROUP, 8, 128), F32),
             pltpu.VMEM((1, WIDE), F32),
             pltpu.VMEM((HALF, 1), F32),
             pltpu.VMEM((WIDE, WIDE), BF16),
@@ -513,8 +578,6 @@
             pltpu.VMEM((2, GROUP, 8, 128), F32),
             pltpu.VMEM((2, GROUP, 8, 128), F32),
             pltpu.VMEM((2, 1, 128), F32),
-            pltpu.VMEM((2, GROUP, 1, 128), F32),
-            pltpu.VMEM((2, 1, 128), F32),
             pltpu.VMEM((GROUP, 1, 128), F32),
             pltpu.VMEM((GROUP, 1, 128), F32),
             pltpu.VMEM((GROUP, WIDE), F32),
@@ -523,6 +586,7 @@
             pltpu.VMEM((GROUP, WIDE), F32),
             pltpu.VMEM((GROUP, WIDE), F32),
             pltpu.VMEM((GROUP, WIDE), F32),
+            pltpu.VMEM((96, HALF), BF16),
             pltpu.VMEM((GROUP, 32, TILE), F32),
             pltpu.VMEM((GROUP, 32, TILE), F32),
             pltpu.VMEM((GROUP, 32, TILE), F32),
@@ -538,17 +602,19 @@
             dma((2,)),
             dma((4,)),
             dma((4,)),
+            dma((GROUP,)),
+            dma((2,)),
             dma((4,)),
-            dma,
-            dma,
-            dma((3, 4)),
-            dma((3, 4)),
+            dma((4,)),
+            dma((3, 3)),
+            dma((3, 3)),
             dma,
             dma((4,)),
             dma,
             dma,
             dma,
             dma((TILES,)),
+            dma,
             dma,
             dma,
         ],

time: 98.6 us -> 88.9 us (0.902)
  Pallas kernels: 97.8 us -> 88 us
    pallas_call x1, Pallas kernels: 96.3 us -> 86.5 us  [body(): pl.pallas_call(kernel, out_shape=jax.ShapeDtypeStruct((CHUNK + 16, FEAT),...]
where the time goes in v4:
time: 88.9 us; the launch traced here: 88.7 us
  Pallas kernels  88 us (99%)
    pallas_call x1, Pallas kernels, body(): pl.pallas_call(kernel, out_shape=jax.ShapeDtypeStruct((CHUNK + 16, FEAT),...  86.5 us

profile of v4, /device:TPU:1, one launch (start us, length us, event | category | flops | bytes accessed | tf_op | source)
XLA Modules:
  0.0 88.7 jit_solution(15087217044500155645)
XLA Ops:
  0.6 86.5 %shard_map.59.joint_ref = f32[80,256]{1,0:T(8,128)} custom-call(bf16[64,256]{1,0:T(8,128)(2,1)} %sup_ref.1, f32[15,64]{1,0:T(8,128)} %lab_ref.1, bf16[32,256,256]{2,1,0:T(8,128)(2,1)} %bitcast.1, f32[15,8192]{1,0:T(8,128)} %tlab_hbm.1), custom_call_target="tpu_custom_call" | custom-call | tf_op jit(solution)/shard_map/pallas_call | solution.py:555
  87.2 1.5 %shard_map.60 = (f32[15,64]{1,0:T(8,128)}, f32[64,256]{1,0:T(8,128)}) custom-call(f32[80,256]{1,0:T(8,128)} %shard_map.59.joint_ref), custom_call_target="tpu_custom_call" | custom-call | tf_op jit(solution)/shard_map/pallas_call | solution.py:625

commit v5 on v4

--- a/solution.py
+++ b/solution.py
@@ -111,7 +111,7 @@
     s1_send, s1_recv, s2_send, s2_rows, s2_cols, t_send, t_rows, t_cols,
     drow, rrow, xrow, dcol, rcol, prev,
     three, both, sib_send, sib_recv, pred_send, pred_recv, err_own, err, xt, gsum, csum, g_send, g_recv,
-    local_sems, f_send, z_recv, x_recv, r_recv, l_send, l_recv, v_send, v_recv,
+    local_sems, f_send, z_recv, x_recv, r_recv, l_send, lz_recv, l_recv, v_send, v_recv,
     sib_ss, sib_rs, pred_ss, pred_rs, err_ss, err_rs, pass_ss, g_ss, g_rs,
 ):
     r = lax.axis_index("row")
@@ -154,7 +154,8 @@
     tlab_copy.start()
 
     barrier = pltpu.get_barrier_semaphore()
-    far_first(4, lambda j: pl.semaphore_signal(barrier, inc=1, device_id=device(zs[j], x), device_id_type=MESH))
+    for d in (1, 3):
+        pl.semaphore_signal(barrier, inc=1, device_id=device(zs[d], x), device_id_type=MESH)
     far_first(4, lambda j: pl.semaphore_signal(barrier, inc=1, device_id=device(z, xs[j]), device_id_type=MESH))
     far_first(
         GROUP, lambda j: pl.semaphore_signal(barrier, inc=1, device_id=row_peer(j)[1], device_id_type=MESH)
@@ -169,7 +170,7 @@
     lab_rows[me] = lab_v[...]
     lab_cols[here] = lab_v[...]
 
-    pl.semaphore_wait(barrier, 21)
+    pl.semaphore_wait(barrier, 20)
 
     drains = []
 
@@ -196,31 +197,40 @@
         remote(cf.at[slot], cf.at[slot], f_send.at[2], x_recv.at[slot], device(z, xs[4 - dx])).start()
 
     col_peers = [(r, ls[j // 4] * 4 + ys[gray(j % 4)]) for j in range(8)]
-    for d in (2, 3, 1):
+    for d in (1, 3):
         remote(sup_v, cf.at[here], f_send.at[0], z_recv.at[z], device(zs[d], x)).start()
     to_x(0, (1, 3))
     for j in range(7, 0, -1):
         remote(sup_v, rf.at[me], f_send.at[1], r_recv.at[0], col_peers[j]).start()
-    for d in (2, 3, 1):
-        remote(lab_v, lab_cols.at[here], l_send.at[0], l_recv.at[0], device(zs[d], x)).start()
+    for d in (1, 3):
+        remote(lab_v, lab_cols.at[here], l_send.at[0], lz_recv.at[z], device(zs[d], x)).start()
     for j in range(7, 0, -1):
         remote(lab_v, lab_rows.at[me], l_send.at[1], l_recv.at[1], col_peers[j]).start()
 
-    for d in (1, 3):
-        wait_for(cf.at[0], z_recv.at[zs[d]])
-        to_x(d, (1, 3))
+    beside = x * 4 + zs[1]
+    wait_for(cf.at[0], z_recv.at[zs[1]])
+    remote(cf.at[beside], cf.at[beside], f_send.at[0], z_recv.at[zs[1]], device(zs[3], x)).start()
+    to_x(1, (1, 3))
+    wait_for(cf.at[0], z_recv.at[zs[3]])
+    to_x(3, (1, 3))
     pass_on(1, 0)
     wait_for(cf.at[0], z_recv.at[zs[2]])
     to_x(2, (1, 3))
+    wait_for(lab_cols.at[0], lz_recv.at[zs[1]])
+    remote(lab_cols.at[beside], lab_cols.at[beside], l_send.at[0], lz_recv.at[zs[1]], device(zs[3], x)).start()
 
     block = pl.ds(core * 8, 8)
     other = 2 * chip + 1 - core
     wait_for(rf.at[pl.ds(0, 7)], r_recv.at[0])
     remote(rf.at[block], rf.at[block], f_send.at[3], r_recv.at[1], (other, c)).start()
-    wait_for(lab_cols.at[pl.ds(0, 3)], l_recv.at[0])
+    pass_on(3, 1)
+    pass_on(3, 3)
+    wait_for(lab_cols.at[0], lz_recv.at[zs[3]])
+    wait_for(lab_cols.at[0], lz_recv.at[zs[2]])
     for d in (2, 3, 1):
         four = lab_cols.at[pl.ds(x * 4, 4)]
         remote(four, four, l_send.at[2], l_recv.at[2], device(z, xs[d])).start()
+    pass_on(1, 2)
     wait_for(lab_rows.at[pl.ds(0, 7)], l_recv.at[1])
     remote(lab_rows.at[block], lab_rows.at[block], l_send.at[3], l_recv.at[3], (other, c)).start()
 
@@ -257,12 +267,6 @@
                 target_tile(2 * i + 1)
 
         done[0] = stop
-
-    fill(4)
-    pass_on(3, 1)
-    pass_on(3, 3)
-    pass_on(1, 2)
-    fill(4)
 
     wait_for(rf.at[pl.ds(0, 8)], r_recv.at[1])
     rn_ref[...] = row_norms(rf[...].reshape(WIDE, FEAT))
@@ -334,7 +338,7 @@
 
     lane = lax.broadcasted_iota(jnp.int32, (1, 128), 1)
     left_half = lax.broadcasted_iota(jnp.int32, (8, 128), 1) < CHUNK
-    waits = ((8, 8), (4, 4))
+    waits = ((0, 12), (6, 14))
     for step in range(3):
         first, last = step == 0, step == 2
         norm = lane_sum(rcol[...] * rcol[...])
@@ -438,6 +442,7 @@
             hi2, mid2, low2 = split3(drow[:, half])
             three[...] = jnp.concatenate([hi, hi2, mid, mid2, low, low2], axis=0)
             predict_theirs()
+            drains.append((sib_recv, sib_ss))
             predict_own()
         else:
             fill(waits[step][1])
@@ -461,7 +466,6 @@
         else:
             pred_recv[chip] = value
 
-    drains.append((sib_recv, sib_ss))
     drains.append((pred_recv.at[pl.ds(0, 15)], pred_ss))
 
     xrow[...] = xrow[...] + alpha * drow[...]
@@ -542,9 +546,14 @@
         wait_for(ref, sem)
 
 
-def part_outputs(joint_ref, coef_ref, grad_ref):
-    coef_ref[...] = joint_ref[CHUNK:CHUNK + 15, 0:CHUNK]
-    grad_ref[...] = joint_ref[0:CHUNK, :]
+def part_outputs(joint_ref, coef_ref, grad_ref, rows, sems):
+    first = pltpu.make_async_copy(joint_ref.at[pl.ds(0, CHUNK)], grad_ref, sems.at[0])
+    second = pltpu.make_async_copy(joint_ref.at[pl.ds(CHUNK, 16)], rows, sems.at[1])
+    first.start()
+    second.start()
+    second.wait()
+    coef_ref[...] = rows[0:15, 0:CHUNK]
+    first.wait()
 
 
 def body(support, support_labels, targets, target_labels):
@@ -606,6 +615,7 @@
             dma((2,)),
             dma((4,)),
             dma((4,)),
+            dma((4,)),
             dma((3, 3)),
             dma((3, 3)),
             dma,
@@ -628,8 +638,10 @@
             jax.ShapeDtypeStruct((classes, CHUNK), F32),
             jax.ShapeDtypeStruct((CHUNK, FEAT), F32),
         ),
-        in_specs=[vmem],
-        out_specs=(vmem, vmem),
+        in_specs=[anywhere],
+        out_specs=(vmem, anywhere),
+        scratch_shapes=[pltpu.VMEM((16, FEAT), F32), dma((2,))],
+        compiler_params=pltpu.CompilerParams(vmem_limit_bytes=58 * 1024 * 1024),
     )(joint)
 
 

time: 88.9 us -> 92.7 us (1.043)
  Pallas kernels: 88 us -> 91.8 us
    pallas_call x1, Pallas kernels: 1.52 us -> 3.7 us  [body(): pl.pallas_call(part_outputs, out_shape=(jax.ShapeDtypeStruct((classes, CH...]
    pallas_call x1, Pallas kernels: 86.5 us -> 88.1 us  [body(): pl.pallas_call(kernel, out_shape=jax.ShapeDtypeStruct((CHUNK + 16, FEAT),...]
where the time goes in v5:
time: 92.7 us; the launch traced here: 92.5 us
  Pallas kernels  91.8 us (99%)
    pallas_call x1, Pallas kernels, body(): pl.pallas_call(kernel, out_shape=jax.ShapeDtypeStruct((CHUNK + 16, FEAT),...  88.1 us
    pallas_call x1, Pallas kernels, body(): pl.pallas_call(part_outputs, out_shape=(jax.ShapeDtypeStruct((classes, CH...  3.7 us

profile of v5, /device:TPU:1, one launch (start us, length us, event | category | flops | bytes accessed | tf_op | source)
XLA Modules:
  0.0 92.5 jit_solution(2128009576220595881)
XLA Ops:
  0.6 88.1 %shard_map.59.joint_ref = f32[80,256]{1,0:T(8,128)} custom-call(bf16[64,256]{1,0:T(8,128)(2,1)} %sup_ref.1, f32[15,64]{1,0:T(8,128)} %lab_ref.1, bf16[32,256,256]{2,1,0:T(8,128)(2,1)} %bitcast.1, f32[15,8192]{1,0:T(8,128)} %tlab_hbm.1), custom_call_target="tpu_custom_call" | custom-call | tf_op jit(solution)/shard_map/pallas_call | solution.py:564
  88.8 3.7 %shard_map.60 = (f32[15,64]{1,0:T(8,128)}, f32[64,256]{1,0:T(8,128)}) custom-call(f32[80,256]{1,0:T(8,128)} %shard_map.59.joint_ref), custom_call_target="tpu_custom_call" | custom-call | tf_op jit(solution)/shard_map/pallas_call | solution.py:635

commit v6 on v4

--- a/solution.py
+++ b/solution.py
@@ -17,6 +17,7 @@
 WIDE = GROUP * CHUNK
 HALF = WIDE // 2
 RIDGE = 0.5
+FILL = (12, 8, 8)
 NN = (((1,), (0,)), ((), ()))
 NT = (((1,), (1,)), ((), ()))
 
@@ -110,7 +111,7 @@
     kt_hi, kt_lo, kk_hi, kk_lo,
     s1_send, s1_recv, s2_send, s2_rows, s2_cols, t_send, t_rows, t_cols,
     drow, rrow, xrow, dcol, rcol, prev,
-    three, both, sib_send, sib_recv, pred_send, pred_recv, err_own, err, xt, gsum, csum, g_send, g_recv,
+    three, one, both, own2, sib_send, sib_recv, sib_send2, sib_recv2, pred_send, pred_recv, err_own, err, xt, gsum, csum, g_send, g_recv,
     local_sems, f_send, z_recv, x_recv, r_recv, l_send, l_recv, v_send, v_recv,
     sib_ss, sib_rs, pred_ss, pred_rs, err_ss, err_rs, pass_ss, g_ss, g_rs,
 ):
@@ -181,24 +182,15 @@
     def wait_for(ref, sem):
         pltpu.make_async_copy(ref, ref, sem).wait()
 
-    def to_x(dz, steps):
+    def to_x(dz):
         slot = xs[0] * 4 + zs[dz]
-        for d in steps:
-            remote(cf.at[slot], cf.at[slot], f_send.at[2], x_recv.at[slot], device(z, xs[d])).start()
-
-    def from_x(dx, dz):
-        slot = xs[dx] * 4 + zs[dz]
-        wait_for(cf.at[0], x_recv.at[slot])
-        return slot
-
-    def pass_on(dx, dz):
-        slot = from_x(dx, dz)
-        remote(cf.at[slot], cf.at[slot], f_send.at[2], x_recv.at[slot], device(z, xs[4 - dx])).start()
+        for d in (2, 1, 3):
+            remote(cf.at[slot], cf.at[slot], f_send.at[2], x_recv.at[x], device(z, xs[d])).start()
 
     col_peers = [(r, ls[j // 4] * 4 + ys[gray(j % 4)]) for j in range(8)]
     for d in (2, 3, 1):
         remote(sup_v, cf.at[here], f_send.at[0], z_recv.at[z], device(zs[d], x)).start()
-    to_x(0, (1, 3))
+    to_x(0)
     for j in range(7, 0, -1):
         remote(sup_v, rf.at[me], f_send.at[1], r_recv.at[0], col_peers[j]).start()
     for d in (2, 3, 1):
@@ -208,10 +200,9 @@
 
     for d in (1, 3):
         wait_for(cf.at[0], z_recv.at[zs[d]])
-        to_x(d, (1, 3))
-    pass_on(1, 0)
+        to_x(d)
     wait_for(cf.at[0], z_recv.at[zs[2]])
-    to_x(2, (1, 3))
+    to_x(2)
 
     block = pl.ds(core * 8, 8)
     other = 2 * chip + 1 - core
@@ -258,33 +249,19 @@
 
         done[0] = stop
 
-    fill(4)
-    pass_on(3, 1)
-    pass_on(3, 3)
-    pass_on(1, 2)
-    fill(4)
+    fill(FILL[0])
 
     wait_for(rf.at[pl.ds(0, 8)], r_recv.at[1])
     rn_ref[...] = row_norms(rf[...].reshape(WIDE, FEAT))
 
     @pl.loop(0, 4)
     def _(i):
-        @pl.when(i == 1)
+        px = lax.rem(x + gray(i), 4)
+
+        @pl.when(i > 0)
         def _():
-            from_x(1, 1)
-            from_x(1, 3)
-
-        @pl.when(i == 2)
-        def _():
-            from_x(3, 0)
-            from_x(3, 2)
-
-        @pl.when(i == 3)
-        def _():
-            for d in range(4):
-                from_x(2, d)
-
-        px = lax.rem(x + gray(i), 4)
+            wait_for(cf.at[pl.ds(0, 4)], x_recv.at[px])
+
         part = cf[pl.ds(px * 4, 4)].reshape(TILE, FEAT)
         inner = dot(part, rf[...].reshape(WIDE, FEAT), NT)
         value = jnp.exp(inner - column_norms(part) - rn_ref[...])
@@ -310,31 +287,42 @@
     rcol[...] = b_cols
     rr = None
 
-    def predict_tile(t):
-        big = dot(three[...], kk_hi[t])
-        small = dot(three[0:64, :], kk_lo[t])
-        return (big[0:32] + small[0:32]) + ((big[32:64] + small[32:64]) + big[64:96])
-
-    def predict_theirs():
+    def predict_tile(t, parts, count):
+        m = 16 * count
+        big = dot(parts[...], kk_hi[t])
+        small = dot(parts[0:2 * m, :], kk_lo[t])
+        return (big[0:m] + small[0:m]) + ((big[m:2 * m] + small[m:2 * m]) + big[2 * m:3 * m])
+
+    def predict_theirs(parts, count, send, recv, which):
         @pl.loop(0, 4)
         def _(g):
             for k in range(4):
                 j = 12 - 4 * g + k
-                sib_send[j] = predict_tile(tile_at(2 * j + 1))
+                send[j] = predict_tile(tile_at(2 * j + 1), parts, count)
             quarter = pl.ds(12 - 4 * g, 4)
-            remote(sib_send.at[quarter], sib_recv.at[quarter], sib_ss, sib_rs.at[3 - g], (other, c)).start()
-
-    def predict_own():
+            remote(send.at[quarter], recv.at[quarter], sib_ss.at[which], sib_rs.at[which, 3 - g], (other, c)).start()
+
+        drains.append((recv, sib_ss.at[which]))
+
+    def predict_own(parts, count, recv, which, store):
         @pl.loop(0, 4)
         def _(g):
-            wait_for(sib_recv.at[pl.ds(0, 4)], sib_rs.at[3 - g])
+            wait_for(recv.at[pl.ds(0, 4)], sib_rs.at[which, 3 - g])
             for k in range(4):
                 j = 12 - 4 * g + k
-                both[j] = predict_tile(tile_at(2 * j)) + sib_recv[j]
+                store[j] = predict_tile(tile_at(2 * j), parts, count) + recv[j]
+
+    def reduce_predictions(which, value):
+        for j in range(GROUP - 1, 0, -1):
+            pred_send[which, j] = value(j)
+            remote(
+                pred_send.at[which, j], pred_recv.at[which, chip], pred_ss.at[which], pred_rs.at[which], col_peer(j)
+            ).start()
+        pred_recv[which, chip] = value(0)
+        drains.append((pred_recv.at[which, pl.ds(0, 15)], pred_ss.at[which]))
 
     lane = lax.broadcasted_iota(jnp.int32, (1, 128), 1)
     left_half = lax.broadcasted_iota(jnp.int32, (8, 128), 1) < CHUNK
-    waits = ((8, 8), (4, 4))
     for step in range(3):
         first, last = step == 0, step == 2
         norm = lane_sum(rcol[...] * rcol[...])
@@ -372,10 +360,16 @@
         far_first(GROUP, send1)
         landed = t_rows.at[pl.ds(0, 15)] if last else s1_recv.at[step, pl.ds(0, 15)]
         drains.append((landed, v_send.at[step, 0]))
-        if last:
+        if first:
+            fill(FILL[1])
+        elif not last:
             fill(TILES)
         else:
-            fill(waits[step][0])
+            hi, mid, low = split3(rrow[:, half])
+            one[...] = jnp.concatenate([hi, mid, low], axis=0)
+            predict_theirs(one, 1, sib_send2, sib_recv2, 1)
+            reduce_predictions(0, lambda j: both[j, 0:16, :] + alpha * both[j, 16:32, :])
+            predict_own(one, 1, sib_recv2, 1, own2)
         wait_for(landed, v_recv.at[step, 0])
         if last:
             scalar_rows = [t_rows[j] for j in range(GROUP)]
@@ -426,6 +420,8 @@
 
             far_first(GROUP, send_rows)
             drains.append((s2_rows.at[step, pl.ds(0, 15)], v_send.at[step, 2]))
+        if last:
+            reduce_predictions(1, lambda j: own2[j] + beta * both[j, 16:32, :])
         if first:
             prev[...] = applied
         else:
@@ -433,14 +429,14 @@
             if not last:
                 prev[...] = applied + beta * prev[...]
                 dcol[...] = rcol[...] + beta * dcol[...]
-        if last:
+        if first:
+            fill(FILL[2])
+        elif not last:
             hi, mid, low = split3(xrow[:, half])
             hi2, mid2, low2 = split3(drow[:, half])
             three[...] = jnp.concatenate([hi, hi2, mid, mid2, low, low2], axis=0)
-            predict_theirs()
-            predict_own()
-        else:
-            fill(waits[step][1])
+            predict_theirs(three, 2, sib_send, sib_recv, 0)
+            predict_own(three, 2, sib_recv, 0, both)
         wait_for(landed, v_recv.at[step, 1])
         if last:
             total = tree([t_cols[j] for j in range(GROUP)])
@@ -452,17 +448,6 @@
             xrow[...] = xrow[...] + alpha * drow[...]
             wait_for(s2_rows.at[step, pl.ds(0, 15)], v_recv.at[step, 2])
             rrow[...] = rrow[...] - alpha * (unpack(s2_rows.at[step]) + RIDGE * drow[...])
-
-    for j in range(GROUP - 1, -1, -1):
-        value = both[j, 0:16, :] + alpha * both[j, 16:32, :]
-        if j > 0:
-            pred_send[j] = value
-            remote(pred_send.at[j], pred_recv.at[chip], pred_ss, pred_rs, col_peer(j)).start()
-        else:
-            pred_recv[chip] = value
-
-    drains.append((sib_recv, sib_ss))
-    drains.append((pred_recv.at[pl.ds(0, 15)], pred_ss))
 
     xrow[...] = xrow[...] + alpha * drow[...]
     pair = xrow[:, pl.ds(pl.multiple_of((me // 2) * 128, 128), 128)]
@@ -477,8 +462,10 @@
     tlab_copy.wait()
     labels = jnp.concatenate([tlab[...], jnp.zeros((1, TILE), F32)], axis=0)
 
-    wait_for(pred_recv.at[pl.ds(0, 15)], pred_rs)
-    own_err = (tree([pred_recv[j] for j in range(GROUP)]) - labels).astype(BF16)
+    for which in range(2):
+        wait_for(pred_recv.at[which, pl.ds(0, 15)], pred_rs.at[which])
+    predictions = tree([pred_recv[0, j] for j in range(GROUP)]) + alpha * tree([pred_recv[1, j] for j in range(GROUP)])
+    own_err = (predictions - labels).astype(BF16)
     err_own[...] = own_err
     err[r] = own_err
 
@@ -587,11 +574,15 @@
             pltpu.VMEM((GROUP, WIDE), F32),
             pltpu.VMEM((GROUP, WIDE), F32),
             pltpu.VMEM((96, HALF), BF16),
+            pltpu.VMEM((48, HALF), BF16),
             pltpu.VMEM((GROUP, 32, TILE), F32),
+            pltpu.VMEM((GROUP, 16, TILE), F32),
             pltpu.VMEM((GROUP, 32, TILE), F32),
             pltpu.VMEM((GROUP, 32, TILE), F32),
             pltpu.VMEM((GROUP, 16, TILE), F32),
             pltpu.VMEM((GROUP, 16, TILE), F32),
+            pltpu.VMEM((2, GROUP, 16, TILE), F32),
+            pltpu.VMEM((2, GROUP, 16, TILE), F32),
             pltpu.VMEM((16, TILE), BF16),
             pltpu.VMEM((TILES, 16, TILE), BF16),
             pltpu.VMEM((HALF, 32), BF16),
@@ -602,16 +593,16 @@
             dma((2,)),
             dma((4,)),
             dma((4,)),
-            dma((GROUP,)),
+            dma((4,)),
             dma((2,)),
             dma((4,)),
             dma((4,)),
             dma((3, 3)),
             dma((3, 3)),
-            dma,
-            dma((4,)),
-            dma,
-            dma,
+            dma((2,)),
+            dma((2, 4)),
+            dma((2,)),
+            dma((2,)),
             dma,
             dma((TILES,)),
             dma,

time: 88.9 us -> 87.9 us (0.989)
  Pallas kernels: 88 us -> 87.1 us
    pallas_call x1, Pallas kernels: 86.5 us -> 85.6 us  [body(): pl.pallas_call(kernel, out_shape=jax.ShapeDtypeStruct((CHUNK + 16, FEAT),...]
where the time goes in v6:
time: 87.9 us; the launch traced here: 87.7 us
  Pallas kernels  87.1 us (99%)
    pallas_call x1, Pallas kernels, body(): pl.pallas_call(kernel, out_shape=jax.ShapeDtypeStruct((CHUNK + 16, FEAT),...  85.6 us

profile of v6, /device:TPU:1, one launch (start us, length us, event | category | flops | bytes accessed | tf_op | source)
XLA Modules:
  0.0 87.7 jit_solution(3814692482927950505)
XLA Ops:
  0.6 85.6 %shard_map.59.joint_ref = f32[80,256]{1,0:T(8,128)} custom-call(bf16[64,256]{1,0:T(8,128)(2,1)} %sup_ref.1, f32[15,64]{1,0:T(8,128)} %lab_ref.1, bf16[32,256,256]{2,1,0:T(8,128)(2,1)} %bitcast.1, f32[15,8192]{1,0:T(8,128)} %tlab_hbm.1), custom_call_target="tpu_custom_call" | custom-call | tf_op jit(solution)/shard_map/pallas_call | solution.py:542
  86.2 1.5 %shard_map.60 = (f32[15,64]{1,0:T(8,128)}, f32[64,256]{1,0:T(8,128)}) custom-call(f32[80,256]{1,0:T(8,128)} %shard_map.59.joint_ref), custom_call_target="tpu_custom_call" | custom-call | tf_op jit(solution)/shard_map/pallas_call | solution.py:616

commit v7 on v6

--- a/solution.py
+++ b/solution.py
@@ -17,7 +17,7 @@
 WIDE = GROUP * CHUNK
 HALF = WIDE // 2
 RIDGE = 0.5
-FILL = (12, 8, 8)
+FILL = (8, 4, 8)
 NN = (((1,), (0,)), ((), ()))
 NT = (((1,), (1,)), ((), ()))
 
@@ -107,11 +107,11 @@
 def kernel(
     sup_ref, lab_ref, tgt_hbm, tlab_hbm,
     out_ref,
-    tgt, tlab, sup_v, lab_v, rf, cf, lab_rows, lab_cols, rn_ref, sn_ref,
+    tgt, tlab, sup_v, lab_v, rf, cf, lab_rows, lab_cols, rn_ref, sn_ref, tn_ref,
     kt_hi, kt_lo, kk_hi, kk_lo,
     s1_send, s1_recv, s2_send, s2_rows, s2_cols, t_send, t_rows, t_cols,
     drow, rrow, xrow, dcol, rcol, prev,
-    three, one, both, own2, sib_send, sib_recv, sib_send2, sib_recv2, pred_send, pred_recv, err_own, err, xt, gsum, csum, g_send, g_recv,
+    three, one, both, own2, sib_send, sib_recv, sib_send2, sib_recv2, u_send, u_recv, w_send, w_recv, pred_send, pred_recv, err_own, err, xt, gsum, csum, g_send, g_recv,
     local_sems, f_send, z_recv, x_recv, r_recv, l_send, l_recv, v_send, v_recv,
     sib_ss, sib_rs, pred_ss, pred_rs, err_ss, err_rs, pass_ss, g_ss, g_rs,
 ):
@@ -198,6 +198,13 @@
     for j in range(7, 0, -1):
         remote(lab_v, lab_rows.at[me], l_send.at[1], l_recv.at[1], col_peers[j]).start()
 
+    tgt_copy.wait()
+
+    @pl.loop(0, TILES // 2)
+    def _(i):
+        tn_ref[2 * i] = row_norms(tgt[2 * i])
+        tn_ref[2 * i + 1] = row_norms(tgt[2 * i + 1])
+
     for d in (1, 3):
         wait_for(cf.at[0], z_recv.at[zs[d]])
         to_x(d)
@@ -226,12 +233,11 @@
 
     half = pl.ds(pl.multiple_of(core * HALF, HALF), HALF)
     sn_ref[...] = column_norms(rf[block].reshape(HALF, FEAT))
-    tgt_copy.wait()
 
     def target_tile(i):
         rows = tgt[i]
         inner = dot(rf[block].reshape(HALF, FEAT), rows, NT)
-        value = jnp.exp(inner - sn_ref[...] - row_norms(rows))
+        value = jnp.exp(inner - sn_ref[...] - tn_ref[i])
         hi = value.astype(BF16)
         kk_hi[i] = hi
         kk_lo[i] = (value - hi.astype(F32)).astype(BF16)
@@ -254,14 +260,10 @@
     wait_for(rf.at[pl.ds(0, 8)], r_recv.at[1])
     rn_ref[...] = row_norms(rf[...].reshape(WIDE, FEAT))
 
-    @pl.loop(0, 4)
-    def _(i):
-        px = lax.rem(x + gray(i), 4)
-
-        @pl.when(i > 0)
-        def _():
+    def system_block(d):
+        px = xs[d]
+        if d:
             wait_for(cf.at[pl.ds(0, 4)], x_recv.at[px])
-
         part = cf[pl.ds(px * 4, 4)].reshape(TILE, FEAT)
         inner = dot(part, rf[...].reshape(WIDE, FEAT), NT)
         value = jnp.exp(inner - column_norms(part) - rn_ref[...])
@@ -269,6 +271,11 @@
         where = pl.ds(pl.multiple_of(px * TILE, TILE), TILE)
         kt_hi[where, :] = hi
         kt_lo[where, :] = (value - hi.astype(F32)).astype(BF16)
+
+    system_block(0)
+    fill(FILL[1])
+    for d in (1, 3, 2):
+        system_block(d)
 
     def apply_tile(v):
         hi, mid, low = split3(v)
@@ -312,14 +319,33 @@
                 j = 12 - 4 * g + k
                 store[j] = predict_tile(tile_at(2 * j), parts, count) + recv[j]
 
-    def reduce_predictions(which, value):
+    def reduce_first(value):
+        for k in range(3, -1, -1):
+            for q in range(4):
+                u_send[k, q] = value(4 * q + k)
+            if k > 0:
+                remote(u_send.at[k], u_recv.at[x], pred_ss.at[0], pred_rs.at[0], device(z, xs[gray(k)])).start()
+            else:
+                u_recv[x] = u_send[0]
+        drains.append((u_recv.at[pl.ds(0, 3)], pred_ss.at[0]))
+
+    def pass_first():
+        wait_for(u_recv.at[pl.ds(0, 3)], pred_rs.at[0])
+        for q in range(3, -1, -1):
+            value = (u_recv[0, q] + u_recv[1, q]) + (u_recv[2, q] + u_recv[3, q])
+            if q > 0:
+                w_send[q] = value
+                remote(w_send.at[q], w_recv.at[z], pred_ss.at[1], pred_rs.at[1], device(zs[gray(q)], x)).start()
+            else:
+                w_recv[z] = value
+        drains.append((w_recv.at[pl.ds(0, 3)], pred_ss.at[1]))
+
+    def reduce_second(value):
         for j in range(GROUP - 1, 0, -1):
-            pred_send[which, j] = value(j)
-            remote(
-                pred_send.at[which, j], pred_recv.at[which, chip], pred_ss.at[which], pred_rs.at[which], col_peer(j)
-            ).start()
-        pred_recv[which, chip] = value(0)
-        drains.append((pred_recv.at[which, pl.ds(0, 15)], pred_ss.at[which]))
+            pred_send[j] = value(j)
+            remote(pred_send.at[j], pred_recv.at[chip], pred_ss.at[2], pred_rs.at[2], col_peer(j)).start()
+        pred_recv[chip] = value(0)
+        drains.append((pred_recv.at[pl.ds(0, 15)], pred_ss.at[2]))
 
     lane = lax.broadcasted_iota(jnp.int32, (1, 128), 1)
     left_half = lax.broadcasted_iota(jnp.int32, (8, 128), 1) < CHUNK
@@ -361,14 +387,17 @@
         landed = t_rows.at[pl.ds(0, 15)] if last else s1_recv.at[step, pl.ds(0, 15)]
         drains.append((landed, v_send.at[step, 0]))
         if first:
-            fill(FILL[1])
+            fill(FILL[2])
         elif not last:
-            fill(TILES)
-        else:
+            hi, mid, low = split3(drow[:, half])
+            hi2, mid2, low2 = split3(rrow[:, half])
+            three[...] = jnp.concatenate([hi, hi2, mid, mid2, low, low2], axis=0)
+            predict_theirs(three, 2, sib_send, sib_recv, 0)
+        else:
+            reduce_first(lambda j: (alpha0 + alpha * beta0) * both[j, 0:16, :] + alpha * both[j, 16:32, :])
             hi, mid, low = split3(rrow[:, half])
             one[...] = jnp.concatenate([hi, mid, low], axis=0)
             predict_theirs(one, 1, sib_send2, sib_recv2, 1)
-            reduce_predictions(0, lambda j: both[j, 0:16, :] + alpha * both[j, 16:32, :])
             predict_own(one, 1, sib_recv2, 1, own2)
         wait_for(landed, v_recv.at[step, 0])
         if last:
@@ -421,7 +450,8 @@
             far_first(GROUP, send_rows)
             drains.append((s2_rows.at[step, pl.ds(0, 15)], v_send.at[step, 2]))
         if last:
-            reduce_predictions(1, lambda j: own2[j] + beta * both[j, 16:32, :])
+            reduce_second(lambda j: own2[j] + beta * (both[j, 16:32, :] + beta0 * both[j, 0:16, :]))
+            pass_first()
         if first:
             prev[...] = applied
         else:
@@ -430,12 +460,8 @@
                 prev[...] = applied + beta * prev[...]
                 dcol[...] = rcol[...] + beta * dcol[...]
         if first:
-            fill(FILL[2])
+            fill(TILES)
         elif not last:
-            hi, mid, low = split3(xrow[:, half])
-            hi2, mid2, low2 = split3(drow[:, half])
-            three[...] = jnp.concatenate([hi, hi2, mid, mid2, low, low2], axis=0)
-            predict_theirs(three, 2, sib_send, sib_recv, 0)
             predict_own(three, 2, sib_recv, 0, both)
         wait_for(landed, v_recv.at[step, 1])
         if last:
@@ -443,6 +469,10 @@
         else:
             total = tree([s2_cols[step, j][7:8] for j in range(GROUP)])
         alpha = ratio(rr, from_lanes(total, CHUNK))
+        if first:
+            alpha0 = alpha
+        elif not last:
+            beta0 = beta
         if not last:
             rcol[...] = rcol[...] - alpha * (unpack(s2_cols.at[step]) + RIDGE * dcol[...])
             xrow[...] = xrow[...] + alpha * drow[...]
@@ -462,9 +492,9 @@
     tlab_copy.wait()
     labels = jnp.concatenate([tlab[...], jnp.zeros((1, TILE), F32)], axis=0)
 
-    for which in range(2):
-        wait_for(pred_recv.at[which, pl.ds(0, 15)], pred_rs.at[which])
-    predictions = tree([pred_recv[0, j] for j in range(GROUP)]) + alpha * tree([pred_recv[1, j] for j in range(GROUP)])
+    wait_for(w_recv.at[pl.ds(0, 3)], pred_rs.at[1])
+    wait_for(pred_recv.at[pl.ds(0, 15)], pred_rs.at[2])
+    predictions = tree([w_recv[j] for j in range(4)]) + alpha * tree([pred_recv[j] for j in range(GROUP)])
     own_err = (predictions - labels).astype(BF16)
     err_own[...] = own_err
     err[r] = own_err
@@ -503,14 +533,14 @@
         return t
 
     zero = jnp.int32(0)
-    add_tiles([take_own(zero), take_own(zero + 1)])
-
-    @pl.loop(1, 8)
+    add_tiles([take_own(zero), take_own(zero + 1), take_own(zero + 2), take_own(zero + 3)])
+
+    @pl.loop(1, 4)
     def _(s):
-        mine = [take_own(2 * s), take_own(2 * s + 1)]
-        add_tiles([take_theirs(2 * s - 2), take_theirs(2 * s - 1)] + mine)
-
-    add_tiles([take_theirs(zero + 14), take_theirs(zero + 15)])
+        mine = [take_own(4 * s + k) for k in range(4)]
+        add_tiles([take_theirs(4 * s - 4 + k) for k in range(4)] + mine)
+
+    add_tiles([take_theirs(zero + 12 + k) for k in range(4)])
     drains.append((err.at[pl.ds(0, 16)], pass_ss))
 
     scale = 1.0 / 256.0
@@ -555,6 +585,7 @@
             pltpu.VMEM((GROUP, 8, 128), F32),
             pltpu.VMEM((1, WIDE), F32),
             pltpu.VMEM((HALF, 1), F32),
+            pltpu.VMEM((TILES, 1, TILE), F32),
             pltpu.VMEM((WIDE, WIDE), BF16),
             pltpu.VMEM((WIDE, WIDE), BF16),
             pltpu.VMEM((TILES, HALF, TILE), BF16),
@@ -581,8 +612,12 @@
             pltpu.VMEM((GROUP, 32, TILE), F32),
             pltpu.VMEM((GROUP, 16, TILE), F32),
             pltpu.VMEM((GROUP, 16, TILE), F32),
-            pltpu.VMEM((2, GROUP, 16, TILE), F32),
-            pltpu.VMEM((2, GROUP, 16, TILE), F32),
+            pltpu.VMEM((4, 4, 16, TILE), F32),
+            pltpu.VMEM((4, 4, 16, TILE), F32),
+            pltpu.VMEM((4, 16, TILE), F32),
+            pltpu.VMEM((4, 16, TILE), F32),
+            pltpu.VMEM((GROUP, 16, TILE), F32),
+            pltpu.VMEM((GROUP, 16, TILE), F32),
             pltpu.VMEM((16, TILE), BF16),
             pltpu.VMEM((TILES, 16, TILE), BF16),
             pltpu.VMEM((HALF, 32), BF16),
@@ -601,8 +636,8 @@
             dma((3, 3)),
             dma((2,)),
             dma((2, 4)),
-            dma((2,)),
-            dma((2,)),
+            dma((3,)),
+            dma((3,)),
             dma,
             dma((TILES,)),
             dma,

time: 87.9 us -> 85.7 us (0.975)
  Pallas kernels: 87.1 us -> 84.8 us
    pallas_call x1, Pallas kernels: 85.6 us -> 83.3 us  [body(): pl.pallas_call(kernel, out_shape=jax.ShapeDtypeStruct((CHUNK + 16, FEAT),...]
where the time goes in v7:
time: 85.7 us; the launch traced here: 85.5 us
  Pallas kernels  84.8 us (99%)
    pallas_call x1, Pallas kernels, body(): pl.pallas_call(kernel, out_shape=jax.ShapeDtypeStruct((CHUNK + 16, FEAT),...  83.3 us

profile of v7, /device:TPU:1, one launch (start us, length us, event | category | flops | bytes accessed | tf_op | source)
XLA Modules:
  0.0 85.5 jit_solution(2514688807677854077)
XLA Ops:
  0.6 83.3 %shard_map.59.joint_ref = f32[80,256]{1,0:T(8,128)} custom-call(bf16[64,256]{1,0:T(8,128)(2,1)} %sup_ref.1, f32[15,64]{1,0:T(8,128)} %lab_ref.1, bf16[32,256,256]{2,1,0:T(8,128)(2,1)} %bitcast.1, f32[15,8192]{1,0:T(8,128)} %tlab_hbm.1), custom_call_target="tpu_custom_call" | custom-call | tf_op jit(solution)/shard_map/pallas_call | solution.py:572
  83.9 1.5 %shard_map.60 = (f32[15,64]{1,0:T(8,128)}, f32[64,256]{1,0:T(8,128)}) custom-call(f32[80,256]{1,0:T(8,128)} %shard_map.59.joint_ref), custom_call_target="tpu_custom_call" | custom-call | tf_op jit(solution)/shard_map/pallas_call | solution.py:651

commit v8 on v7

--- a/solution.py
+++ b/solution.py
@@ -17,7 +17,7 @@
 WIDE = GROUP * CHUNK
 HALF = WIDE // 2
 RIDGE = 0.5
-FILL = (8, 4, 8)
+FILL = (2, 2, 8, 16)
 NN = (((1,), (0,)), ((), ()))
 NT = (((1,), (1,)), ((), ()))
 
@@ -392,6 +392,7 @@
             hi, mid, low = split3(drow[:, half])
             hi2, mid2, low2 = split3(rrow[:, half])
             three[...] = jnp.concatenate([hi, hi2, mid, mid2, low, low2], axis=0)
+            fill(TILES)
             predict_theirs(three, 2, sib_send, sib_recv, 0)
         else:
             reduce_first(lambda j: (alpha0 + alpha * beta0) * both[j, 0:16, :] + alpha * both[j, 16:32, :])
@@ -460,7 +461,7 @@
                 prev[...] = applied + beta * prev[...]
                 dcol[...] = rcol[...] + beta * dcol[...]
         if first:
-            fill(TILES)
+            fill(FILL[3])
         elif not last:
             predict_own(three, 2, sib_recv, 0, both)
         wait_for(landed, v_recv.at[step, 1])

time: 85.7 us -> 83.6 us (0.975)
  Pallas kernels: 84.8 us -> 82.7 us
    pallas_call x1, Pallas kernels: 83.3 us -> 81.2 us  [body(): pl.pallas_call(kernel, out_shape=jax.ShapeDtypeStruct((CHUNK + 16, FEAT),...]
where the time goes in v8:
time: 83.6 us; the launch traced here: 83.4 us
  Pallas kernels  82.7 us (99%)
    pallas_call x1, Pallas kernels, body(): pl.pallas_call(kernel, out_shape=jax.ShapeDtypeStruct((CHUNK + 16, FEAT),...  81.2 us

profile of v8, /device:TPU:1, one launch (start us, length us, event | category | flops | bytes accessed | tf_op | source)
XLA Modules:
  0.0 83.4 jit_solution(1370148719789093564)
XLA Ops:
  0.6 81.2 %shard_map.59.joint_ref = f32[80,256]{1,0:T(8,128)} custom-call(bf16[64,256]{1,0:T(8,128)(2,1)} %sup_ref.1, f32[15,64]{1,0:T(8,128)} %lab_ref.1, bf16[32,256,256]{2,1,0:T(8,128)(2,1)} %bitcast.1, f32[15,8192]{1,0:T(8,128)} %tlab_hbm.1), custom_call_target="tpu_custom_call" | custom-call | tf_op jit(solution)/shard_map/pallas_call | solution.py:573
  81.8 1.5 %shard_map.60 = (f32[15,64]{1,0:T(8,128)}, f32[64,256]{1,0:T(8,128)}) custom-call(f32[80,256]{1,0:T(8,128)} %shard_map.59.joint_ref), custom_call_target="tpu_custom_call" | custom-call | tf_op jit(solution)/shard_map/pallas_call | solution.py:652

commit v9 on v8

--- a/solution.py
+++ b/solution.py
@@ -17,7 +17,7 @@
 WIDE = GROUP * CHUNK
 HALF = WIDE // 2
 RIDGE = 0.5
-FILL = (2, 2, 8, 16)
+FILL = (0, 2, 6, 14, 4)
 NN = (((1,), (0,)), ((), ()))
 NT = (((1,), (1,)), ((), ()))
 
@@ -234,7 +234,9 @@
     half = pl.ds(pl.multiple_of(core * HALF, HALF), HALF)
     sn_ref[...] = column_norms(rf[block].reshape(HALF, FEAT))
 
-    def target_tile(i):
+    def target_tile(n):
+        own = n // GROUP
+        i = 2 * (n - GROUP * own) + (1 - core) + own * (2 * core - 1)
         rows = tgt[i]
         inner = dot(rf[block].reshape(HALF, FEAT), rows, NT)
         value = jnp.exp(inner - sn_ref[...] - tn_ref[i])
@@ -392,7 +394,7 @@
             hi, mid, low = split3(drow[:, half])
             hi2, mid2, low2 = split3(rrow[:, half])
             three[...] = jnp.concatenate([hi, hi2, mid, mid2, low, low2], axis=0)
-            fill(TILES)
+            fill(FILL[4])
             predict_theirs(three, 2, sib_send, sib_recv, 0)
         else:
             reduce_first(lambda j: (alpha0 + alpha * beta0) * both[j, 0:16, :] + alpha * both[j, 16:32, :])
@@ -463,6 +465,7 @@
         if first:
             fill(FILL[3])
         elif not last:
+            fill(TILES)
             predict_own(three, 2, sib_recv, 0, both)
         wait_for(landed, v_recv.at[step, 1])
         if last:

time: 83.6 us -> 83.4 us (level)
  no operation moved by 1% of the time
where the time goes in v9:
time: 83.4 us; the launch traced here: 83.2 us
  Pallas kernels  82.6 us (99%)
    pallas_call x1, Pallas kernels, body(): pl.pallas_call(kernel, out_shape=jax.ShapeDtypeStruct((CHUNK + 16, FEAT),...  81 us

profile of v9, /device:TPU:1, one launch (start us, length us, event | category | flops | bytes accessed | tf_op | source)
XLA Modules:
  0.0 83.2 jit_solution(5308576100084992094)
XLA Ops:
  0.6 81.0 %shard_map.59.joint_ref = f32[80,256]{1,0:T(8,128)} custom-call(bf16[64,256]{1,0:T(8,128)(2,1)} %sup_ref.1, f32[15,64]{1,0:T(8,128)} %lab_ref.1, bf16[32,256,256]{2,1,0:T(8,128)(2,1)} %bitcast.1, f32[15,8192]{1,0:T(8,128)} %tlab_hbm.1), custom_call_target="tpu_custom_call" | custom-call | tf_op jit(solution)/shard_map/pallas_call | solution.py:576
  81.7 1.5 %shard_map.60 = (f32[15,64]{1,0:T(8,128)}, f32[64,256]{1,0:T(8,128)}) custom-call(f32[80,256]{1,0:T(8,128)} %shard_map.59.joint_ref), custom_call_target="tpu_custom_call" | custom-call | tf_op jit(solution)/shard_map/pallas_call | solution.py:655
